TPU v7x, 32 devices: a whole 2x2x4 slice. The times are simulated.
32 devices in a mesh: dom: 8 (over z, x), rep: 4 (over y, core).
Axes of the slice: x: 2, y: 2, z: 4, core: 2. Of those that a mesh axis runs over, the one named last changes fastest.
Arguments:
- feats: bfloat16 [32768, 256], P(('dom', 'rep')), may hold values from -6 to 6
- w_self: bfloat16 [256, 256], replicated, may hold values from -0.375 to 0.375
- w_neigh: bfloat16 [256, 256], replicated, may hold values from -0.375 to 0.375
- bias: float32 [256], replicated, may hold values from -3 to 3
- out_cot: bfloat16 [32768, 256], P(('dom', 'rep')), may hold values from -6 to 6
- degree: int32 [32768], P(('dom', 'rep')), may hold values from 1 to 20
- edge_src: int32 [32768, 10], P(('dom', 'rep')), may hold values from 0 to 1119, as said below
- hub_rows: int32 [64], P(('dom', 'rep')), may hold values from 0 to 1023, as said below
- send_rows: int32 [256, 4], P(('dom', 'rep')), may hold values from -1 to 1023, as said below
Outputs:
- outputs: bfloat16 [32768, 256], P(('dom', 'rep'))
- grad_feats: bfloat16 [32768, 256], P(('dom', 'rep'))
- unit_w_self: float32 [256, 256], replicated
- unit_w_neigh: float32 [256, 256], replicated
- unit_bias: float32 [256], replicated
Inputs may be any that keep to these rules, and one draw needn't show every extreme that they name: `hub_rows`: the 2 entries of one block are distinct rows of that block. `send_rows`: row q * 8 + e lists rows of block q for partition e: live entries first, then -1; every list has a live entry, every block has a full list, and one partition receives full lists from all blocks. `edge_src`: A slot of the halo part of a block's table always names a live entry of the list it comes from.
All inputs are finite; a program needn't handle non-finite values.
Results may differ from a plain program's by a relative error of at most 0.0056.
Values may be sent and summed in bfloat16 or wider, within the bound.
No kernel may reach another device: no remote copies, remote signals or barrier semaphores. Data moves between devices by JAX's collectives and lax.ppermute only.
A program may use at most 128 MiB of HBM per device.

v0:
```python
import functools

import jax
import jax.numpy as jnp
from jax import lax
from jax.experimental import pallas as pl
from jax.experimental.pallas import tpu as pltpu
from jax.sharding import PartitionSpec as P

NORM_EPS = 1e-05
UNIT_EPS = 1e-06
SPLIT_AXES = ("dom", "pair", "side")
PEERS = ("dom", "pair")
SIDES = 2
VMEM_LIMIT = 32 * 1024 * 1024
F32 = jnp.float32
BF16 = jnp.bfloat16
TILE = 256
STRIP = 16
PIECE = 32
LANES = 128
BIAS_ROWS = 2


def div_floor(value, size):
    if size & (size - 1) == 0:
        return lax.shift_right_arithmetic(value, jnp.int32(size.bit_length() - 1))
    return value // size


def remainder(value, size):
    if size & (size - 1) == 0:
        return value & jnp.int32(size - 1)
    return value - (value // size) * size


def matmul(lhs, rhs, lhs_dim=1, rhs_dim=0):
    return lax.dot_general(
        lhs, rhs, (((lhs_dim,), (rhs_dim,)), ((), ())), preferred_element_type=F32
    )


def iota(shape, dim):
    return lax.broadcasted_iota(jnp.int32, shape, dim)


def one_hot(rows, places):
    return jnp.where(iota((rows, places.shape[1]), 0) == places, F32(1.0), F32(0.0)).astype(BF16)


def fetch(pairs, sems):
    copies = [
        pltpu.make_async_copy(source, target, sems.at[number])
        for number, (source, target) in enumerate(pairs)
    ]
    for copy in copies:
        copy.start()
    return copies


def pick_kernel(sizes, hub_hbm, send_hbm, *refs):
    doms, reps, cap, hub_own, tall = sizes
    inputs, (rows_ref, hubs_ref, places_ref), kept, (hub_ref, send_ref, sems) = (
        refs[:5],
        refs[5:8],
        refs[8:13],
        refs[13:],
    )
    feats_ref = kept[0]
    copies = fetch(((hub_hbm, hub_ref), (send_hbm, send_ref), *zip(inputs, kept)), sems)
    slots = doms * tall
    lane = iota(places_ref.shape, 1)
    row = remainder(lane, tall)

    def list_entries(dom, places):
        for entry in range(cap):
            places = jnp.where(lane == dom * tall + entry, send_ref[entry, dom], places)
        return places

    copies[0].wait()
    copies[1].wait()
    places = jnp.full(lane.shape, -1, jnp.int32)
    if doms <= 16:
        for dom in range(doms):
            places = list_entries(dom, places)
    else:
        places = lax.fori_loop(0, doms, list_entries, places)
    for entry in range(hub_own):
        for first, inside in ((cap, lane < slots), (cap + hub_own, lane >= slots)):
            places = jnp.where((row == first + entry) & inside, hub_ref[entry], places)
    places_ref[...] = places
    column = jnp.broadcast_to(places, (LANES, lane.shape[1])).T[: slots + 2 * tall, :]
    node = iota(column.shape, 1)
    chosen = [
        jnp.where(node + first == column, F32(1.0), F32(0.0)).astype(BF16)
        for first in range(0, feats_ref.shape[0], LANES)
    ]
    copies[2].wait()
    picked = matmul(jnp.concatenate(chosen, axis=1), feats_ref[...]).astype(BF16)
    rows_ref[...] = picked[:slots, :]
    hubs_ref[...] = picked[slots:, :]
    for copy in copies[3:]:
        copy.wait()


def message_kernel(sizes, rows_ref, hubs_ref, after_ref, message_ref):
    doms, reps, cap, hub_own, tall = sizes
    del after_ref
    rows = rows_ref[...].astype(F32)
    hubs = hubs_ref[...].astype(F32)[:tall, :]
    place = iota(hubs.shape, 0)
    pair = lax.axis_index("pair")
    pairs = reps // SIDES
    for dom in range(doms):
        block = rows[dom * tall : (dom + 1) * tall, :]
        blocks = [
            jnp.where((place >= cap) | (pair == other), block, F32(0.0)) + hubs
            for other in range(pairs)
        ]
        first = dom * pairs * tall
        message_ref[first : first + pairs * tall, :] = jnp.concatenate(blocks, axis=0).astype(BF16)


def count_edges(slot_ref, own_count_ref, far_count_ref, hot_ref, nodes):
    fanout, rows = slot_ref.shape[0], own_count_ref.shape[0]
    highs = (rows + far_count_ref.shape[0]) // LANES
    low, high = [], []
    for k in range(fanout):
        slot = jnp.broadcast_to(slot_ref[k : k + 1, nodes], (STRIP, TILE))
        low.append(remainder(slot, LANES).astype(jnp.int16))
        high.append(div_floor(slot, LANES).astype(jnp.int16))
    for block in range(highs):
        for k in range(fanout):
            hot_ref[block * fanout + k] = jnp.where(high[k] == block, BF16(1.0), BF16(0.0))
    for strip in range(0, LANES, STRIP):
        numbers = (iota((STRIP, TILE), 0) + strip).astype(jnp.int16)
        hot = [jnp.where(numbers == low[k], BF16(1.0), BF16(0.0)) for k in range(fanout)]
        for block in range(highs):
            count = hot[0] * hot_ref[block * fanout]
            for k in range(1, fanout):
                count = count + hot[k] * hot_ref[block * fanout + k]
            first = block * LANES + strip
            if first < rows:
                own_count_ref[first : first + STRIP, nodes] = count
            else:
                far_count_ref[first - rows : first - rows + STRIP, nodes] = count


def own_kernel(sizes, feats_ref, w_self_ref, bias_ref, degree_ref, edge_ref, *refs):
    doms, reps, cap, hub_own, tall = sizes
    inputs, refs = refs[:2], refs[2:]
    kept, (share_ref, turned_ref, own_count_ref, far_count_ref, total_ref, preact_ref) = (
        refs[:2],
        refs[2:8],
    )
    slot_ref, hot_ref, sems = refs[8:]
    copies = fetch(zip(inputs, kept), sems)
    rows = feats_ref.shape[0]
    fanout = edge_ref.shape[0]
    hubs = doms * reps * hub_own

    source = edge_ref[...]
    hub = source - rows
    halo = hub - hubs
    chip = SIDES * hub_own
    entry = remainder(hub, chip) ^ (lax.axis_index("side") * hub_own)
    hub_slot = rows + cap + div_floor(hub, chip) * tall + entry
    peer = div_floor(halo, cap) * (reps // SIDES) + lax.axis_index("pair")
    halo_slot = rows + peer * tall + remainder(halo, cap)
    slot = jnp.where(source < rows, source, jnp.where(hub < hubs, hub_slot, halo_slot))
    valid = jnp.minimum(degree_ref[...], fanout)
    slot_ref[...] = jnp.where(iota((fanout, rows), 0) < valid, slot, -1)
    share_ref[...] = 1.0 / valid.astype(F32)
    turned_ref[...] = feats_ref[...].T

    def own_sums(nodes):
        total_ref[:, nodes] = matmul(turned_ref[...], own_count_ref[:, nodes])
        preact_ref[nodes, :] = matmul(feats_ref[nodes, :], w_self_ref[...]) + bias_ref[...]

    if rows + far_count_ref.shape[0] > 2048:

        @pl.loop(0, rows, step=TILE)
        def node_tile(first):
            nodes = pl.ds(pl.multiple_of(first, TILE), TILE)
            count_edges(slot_ref, own_count_ref, far_count_ref, hot_ref.at[0], nodes)
            own_sums(nodes)

    else:
        counted = None
        for number in range(rows // TILE):
            nodes = slice(number * TILE, (number + 1) * TILE)
            count_edges(slot_ref, own_count_ref, far_count_ref, hot_ref.at[number % 2], nodes)
            if counted is not None:
                own_sums(counted)
            counted = nodes
        own_sums(counted)
    for copy in copies:
        copy.wait()


def joint_kernel(
    sizes,
    remote_ref,
    turned_ref,
    total_ref,
    self_ref,
    count_ref,
    share_ref,
    w_neigh_ref,
    cot_ref,
    outputs_hbm,
    w_own_ref,
    rest_ref,
    message_ref,
    low_ref,
    edge_grad_ref,
    bias_ref,
    outputs_ref,
    mean_ref,
    preact_ref,
    w_grad_ref,
    sems,
):
    doms, reps, cap, hub_own, tall = sizes
    rows, width = outputs_ref.shape
    tiles = [slice(first, first + TILE) for first in range(0, rows, TILE)]
    table = remote_ref[...].T

    def before_head(nodes):
        mean = total_ref[:, nodes] + matmul(table, count_ref[:, nodes])
        mean = (mean * share_ref[:, nodes]).astype(BF16)
        mean_ref[:, nodes] = mean
        preact_ref[nodes, :] = self_ref[nodes, :] + matmul(mean, w_neigh_ref[...], 0, 0)

    bias_sum = jnp.zeros((8, width), F32)
    copies = []
    before_head(tiles[0])
    for number, nodes in enumerate(tiles):
        if number + 1 < len(tiles):
            before_head(tiles[number + 1])
        for start in range(nodes.start, nodes.stop, PIECE):
            piece = slice(start, start + PIECE)
            preact = preact_ref[piece, :]
            cot = cot_ref[piece, :].astype(F32)
            grown = jnp.exp(jnp.minimum(preact, 0.0))
            act = jnp.where(preact > 0.0, preact, grown - 1.0)
            square = jnp.sum(act * act, axis=1, keepdims=True)
            along = jnp.sum(act * cot, axis=1, keepdims=True)
            scale = lax.rsqrt(square * (1.0 / width) + NORM_EPS)
            outputs_ref[piece, :] = (act * scale).astype(BF16)
            pull = along * (scale * scale * scale) * (1.0 / width)
            grad_pre = (cot * scale - act * pull) * jnp.where(preact > 0.0, F32(1.0), grown)
            bias_sum = bias_sum + jnp.sum(grad_pre.reshape(PIECE // 8, 8, width), axis=0)
            low_ref[piece, :] = grad_pre.astype(BF16)
        copies += fetch(
            ((outputs_ref.at[nodes, :], outputs_hbm.at[nodes, :]),), sems.at[pl.ds(number, 1)]
        )
        share_column = jnp.broadcast_to(share_ref[:, nodes], (LANES, TILE)).T
        share_column = jnp.concatenate([share_column] * (width // LANES), axis=1)
        edge_grad = matmul(low_ref[nodes, :], w_neigh_ref[...], 1, 1) * share_column
        edge_grad_ref[nodes, :] = edge_grad.astype(BF16)

    w_grad_ref[0] = matmul(turned_ref[...], low_ref[...])
    w_grad_ref[1] = matmul(mean_ref[...], low_ref[...])
    remote = matmul(count_ref[...], edge_grad_ref[...])
    rest_ref[...] = remote
    bias_ref[...] = bias_sum
    bias_sum = jnp.broadcast_to(jnp.sum(bias_sum, axis=0, keepdims=True), (tall, width))
    bias_high = bias_sum.astype(BF16).astype(F32)
    place = iota((tall, width), 0)
    bias_rows = jnp.where(place == cap, bias_high, bias_sum - bias_high)
    bias_rows = jnp.where(place < cap, F32(0.0), bias_rows)
    message = remote.reshape(-1, tall, width)
    message = jnp.where((place < cap + hub_own)[None], bias_rows[None], message)
    message_ref[width:, :] = message.reshape(remote.shape).astype(BF16)
    mine = lax.axis_index("side")
    w_own_ref[...] = w_grad_ref[mine]
    message_ref[:width, :] = w_grad_ref[1 - mine].astype(BF16)
    for copy in copies:
        copy.wait()


def own_grad_kernel(low_ref, w_self_ref, own_count_ref, edge_grad_ref, feat_grad_ref):
    for first in range(0, low_ref.shape[0], TILE):
        nodes = slice(first, first + TILE)
        feat_grad_ref[nodes, :] = matmul(own_count_ref[nodes, :], edge_grad_ref[...]) + matmul(
            low_ref[nodes, :], w_self_ref[...], 1, 1
        )


def side_sum_kernel(own_ref, received_ref, after_ref, message_ref):
    del after_ref
    peers, slab, width = message_ref.shape
    w_grad = own_ref[...] + received_ref[:width, :].astype(F32)
    owners = width // slab
    w_grad = w_grad.reshape(owners, slab, width)
    if owners < peers:
        w_grad = jnp.concatenate([w_grad, jnp.zeros((peers - owners, slab, width), F32)], axis=0)
    message_ref[...] = w_grad.astype(BF16)


def peer_sum_kernel(sizes, slabs_ref, own_ref, received_ref, bias_ref, message_ref):
    doms, reps, cap, hub_own, tall = sizes
    peers, slab, width = slabs_ref.shape
    total = jnp.sum(slabs_ref[...].astype(F32), axis=0)
    received_ref = received_ref.at[width:, :]
    size = min(peers * tall, LANES)
    to, source = iota((size, size), 0), iota((size, size), 1)
    entry = remainder(to, tall) - cap
    moved = (source == to + hub_own) & (entry >= 0) & (entry < hub_own)
    moved = jnp.where(moved, F32(1.0), F32(0.0)).astype(BF16)
    rest = own_ref[...] + jnp.concatenate(
        [
            matmul(moved, received_ref[first : first + size, :])
            for first in range(0, peers * tall, size)
        ],
        axis=0,
    )
    place = iota((tall, width), 0)
    bias = received_ref[: 2 * tall, :].astype(F32)[:tall, :]
    bias = jnp.where((place >= cap) & (place < cap + BIAS_ROWS), bias, F32(0.0)) + bias_ref[...]
    bias = jnp.broadcast_to(jnp.sum(bias, axis=0, keepdims=True), (tall, width))
    bias_high = bias.astype(BF16).astype(F32)
    bias_rows = jnp.where(place == tall - 1, bias - bias_high, bias_high)
    rest = rest.reshape(peers, tall, width)
    rest = jnp.where((place < tall - BIAS_ROWS)[None], rest, bias_rows[None])
    total = jnp.broadcast_to(total[None], (peers, slab, width))
    message_ref[...] = jnp.concatenate([total, rest], axis=1).astype(BF16)


def feat_grad_kernel(sizes, slab, message_ref, places_ref, feat_grad_ref, out_ref):
    doms, reps, cap, hub_own, tall = sizes
    rows, width = out_ref.shape
    pairs = reps // SIDES
    returned = message_ref[...].astype(F32)[:, slab:, :].reshape(doms, pairs, tall, width)
    returned = [
        returned[:, pair].reshape(doms * tall, width).astype(BF16) for pair in range(pairs)
    ]
    chosen = one_hot(rows, places_ref[:, : doms * tall])
    for first in range(0, rows, TILE):
        nodes = slice(first, first + TILE)
        total = feat_grad_ref[nodes, :]
        for part in returned:
            total = total + matmul(chosen[nodes, :], part)
        out_ref[nodes, :] = total.astype(BF16)


def unit_kernel(slab, mine_ref, other_ref, unit_self_ref, unit_neigh_ref, unit_bias_ref, units_ref):
    side = lax.axis_index("side")
    size, width = unit_self_ref.shape
    for place, grad_ref in ((side, mine_ref), (1 - side, other_ref)):
        grad = grad_ref[: size // slab].astype(F32)[:, :slab, :].reshape(size, width)
        square = jnp.sum(jnp.sum(grad * grad, axis=0, keepdims=True), axis=1, keepdims=True)
        units_ref[place] = grad * lax.rsqrt(square * (1.0 / grad.size) + UNIT_EPS)
    unit_self_ref[...] = units_ref[0]
    unit_neigh_ref[...] = units_ref[1]
    bias = jnp.sum(mine_ref[...].astype(F32)[:, slab:, :], axis=0)[-BIAS_ROWS:, :]
    bias = jnp.sum(bias, axis=0, keepdims=True)
    unit_bias_ref[...] = bias * lax.rsqrt(jnp.mean(bias * bias, axis=1, keepdims=True) + UNIT_EPS)


def call(kernel, out_shape, in_specs=None, scratch=(), cost=(0, 0), out_specs=None):
    specs = {"in_specs": in_specs, "out_specs": out_specs}
    return pl.pallas_call(
        kernel,
        out_shape=out_shape,
        **{name: spec for name, spec in specs.items() if spec is not None},
        scratch_shapes=list(scratch),
        compiler_params=pltpu.CompilerParams(vmem_limit_bytes=VMEM_LIMIT),
        cost_estimate=pl.CostEstimate(flops=cost[0], bytes_accessed=cost[1], transcendentals=0),
    )


def in_hbm(*arrays):
    return [pltpu.with_memory_space_constraint(array, pltpu.HBM) for array in arrays]


def swap(array, axes):
    return lax.all_to_all(array, axes, split_axis=0, concat_axis=0, tiled=True)


def other_side(array):
    return lax.ppermute(array, "side", [(0, 1), (1, 0)])


def on_device(
    doms, reps, feats, w_self, w_neigh, bias, out_cot, degree, edge_src, hub_rows, send_rows
):
    rows, width = feats.shape
    fanout = edge_src.shape[1]
    cap, hub_own = send_rows.shape[1], hub_rows.shape[0]
    peers = doms * reps // SIDES
    tall = cap + SIDES * hub_own
    if tall % 8 or tall < cap + hub_own + BIAS_ROWS or hub_own & (hub_own - 1):
        raise ValueError("message height")
    slots = peers * tall
    slab = max(8, width // peers)
    sizes = (doms, reps, cap, hub_own, tall)
    shape = jax.ShapeDtypeStruct
    hbm = pl.BlockSpec(memory_space=pltpu.HBM)
    vmem = pl.BlockSpec(memory_space=pltpu.VMEM)

    picked, hubs, places, *kept = call(
        functools.partial(pick_kernel, sizes),
        (
            shape((doms * tall, width), BF16),
            shape((2 * tall, width), BF16),
            shape((1, -(-(doms + 2) * tall // LANES) * LANES), jnp.int32),
            shape((rows, width), BF16),
            shape((width, width), BF16),
            shape((1, width), F32),
            shape((1, rows), jnp.int32),
            shape((fanout, rows), jnp.int32),
        ),
        [hbm] * 7,
        (
            pltpu.SMEM((hub_own,), jnp.int32),
            pltpu.SMEM((cap, doms), jnp.int32),
            pltpu.SemaphoreType.DMA((7,)),
        ),
        cost=(2 * rows * slots * width, 2 * rows * width),
    )(
        *in_hbm(
            hub_rows,
            send_rows.T,
            feats,
            w_self,
            bias.reshape(1, width),
            degree.reshape(1, rows),
            edge_src.T,
        )
    )
    hubs = other_side(hubs)
    w_neigh_kept, cot_kept, share, turned, own_count, far_count, own_total, self_part = call(
        functools.partial(own_kernel, sizes),
        (
            shape((width, width), BF16),
            shape((rows, width), BF16),
            shape((1, rows), F32),
            shape((width, rows), BF16),
            shape((rows, rows), BF16),
            shape((slots, rows), BF16),
            shape((width, rows), F32),
            shape((rows, width), F32),
        ),
        [vmem] * 5 + [hbm] * 2,
        (
            pltpu.VMEM((fanout, rows), jnp.int32),
            pltpu.VMEM((2, (rows + slots) // LANES * fanout, STRIP, TILE), BF16),
            pltpu.SemaphoreType.DMA((2,)),
        ),
        cost=(8 * rows * (rows + slots) * width, 12 * rows * width + 2 * rows * rows),
    )(*kept, *in_hbm(w_neigh, out_cot))

    message = call(
        functools.partial(message_kernel, sizes),
        shape((slots, width), BF16),
        [vmem, vmem, pl.BlockSpec(memory_space=pl.ANY)],
    )(picked, hubs, share)
    remote = swap(message, PEERS)

    outputs, w_own, rest, message, low, edge_grad, bias_sum = call(
        functools.partial(joint_kernel, sizes),
        (
            pltpu.HBM((rows, width), BF16),
            shape((width, width), F32),
            shape((slots, width), F32),
            shape((width + slots, width), BF16),
            shape((rows, width), BF16),
            shape((rows, width), BF16),
            shape((8, width), F32),
        ),
        out_specs=(hbm,) + (vmem,) * 6,
        scratch=(
            pltpu.VMEM((rows, width), BF16),
            pltpu.VMEM((width, rows), BF16),
            pltpu.VMEM((rows, width), F32),
            pltpu.VMEM((2, width, width), F32),
            pltpu.SemaphoreType.DMA((rows // TILE,)),
        ),
        cost=(4 * rows * slots * width + 8 * rows * width * width, 16 * rows * width),
    )(remote, turned, own_total, self_part, far_count, share, w_neigh_kept, cot_kept)

    received = other_side(message)
    feat_grad = call(
        own_grad_kernel,
        shape((rows, width), F32),
        cost=(2 * rows * rows * width + 2 * rows * width * width, 8 * rows * width),
    )(low, kept[1], own_count, edge_grad)
    message = call(
        side_sum_kernel,
        shape((peers, slab, width), BF16),
        [vmem, vmem, pl.BlockSpec(memory_space=pl.ANY)],
    )(w_own, received, feat_grad)
    slabs = swap(message, PEERS)
    message = call(
        functools.partial(peer_sum_kernel, sizes), shape((peers, slab + tall, width), BF16)
    )(slabs, rest, received, bias_sum)
    message = swap(message, PEERS)
    grad_feats = call(
        functools.partial(feat_grad_kernel, sizes, slab),
        shape((rows, width), BF16),
        cost=(4 * rows * slots * width, 6 * rows * width),
    )(message, places, feat_grad)
    unit_self, unit_neigh, unit_bias = call(
        functools.partial(unit_kernel, slab),
        (shape((width, width), F32), shape((width, width), F32), shape((1, width), F32)),
        scratch=(pltpu.VMEM((2, width, width), F32),),
    )(message, other_side(message))
    return outputs, grad_feats, unit_self, unit_neigh, unit_bias.reshape(width)


def solution(mesh):
    doms, reps = mesh.shape["dom"], mesh.shape["rep"]
    split = jax.sharding.Mesh(mesh.devices.reshape(doms, reps // SIDES, SIDES), SPLIT_AXES)
    rows, whole = P(SPLIT_AXES, None), P()
    return jax.shard_map(
        functools.partial(on_device, doms, reps),
        mesh=split,
        in_specs=(rows, whole, whole, whole, rows, P(SPLIT_AXES), rows, P(SPLIT_AXES), rows),
        out_specs=(rows, rows, whole, whole, whole),
        check_vma=False,
    )
```

profile of v0, /device:TPU:0, one launch (start us, length us, event | category | flops | bytes accessed | tf_op | source)
XLA Modules:
  0.0 49.1 jit_solution(2393785949635567670)
XLA Ops:
  0.6 1.3 %shard_map.128 = (bf16[64,256]{1,0:T(8,128)(2,1)S(1)}, bf16[16,256]{1,0:T(8,128)(2,1)S(1)}, s32[1,128]{1,0:T(1,128)S(1)}, bf16[1024,256]{1,0:T(8,128)(2,1)S(1)},...) custom-call(s32[2]{0:T(128)} %hub_hbm.1, ...), custom_call_target="tpu_custom_call" | custom-call | flops 67108864 | bytes 524288 | tf_op jit(solution)/shard_map/pallas_call | solution.py:403
  2.0 0.5 %collective-permute-start = (bf16[16,256]{1,0:T(8,128)(2,1)S(1)}, bf16[16,256]{1,0:T(8,128)(2,1)S(1)}, u32[]{:S(2)}, u32[]{:S(2)}) collective-permute-start(bf16[16,256]{1,0:T(8,128)(2,1)S(1)} %get-tuple-element.32), channel_id=1, source_target_pairs={{0,1},{1,0},{2,3},{3,2},{4,5},{5,4},{6,7},{7,6},{8,9},{9,8},{10,11... | collective-permute-start | bytes 24584 | tf_op jit(solution)/shard_map/ppermute | solution.py:383
  2.5 2.7 %shard_map.129 = (bf16[256,256]{1,0:T(8,128)(2,1)S(1)}, bf16[1024,256]{1,0:T(8,128)(2,1)S(1)}, f32[1,1024]{1,0:T(1,128)S(1)}, bf16[256,1024]{1,0:T(8,128)(2,1)S(...) custom-call(bf16[1024,256]{1,0:T(8,128)(2,1)S(1)} %get-tuple-element, ...), custom_call_target="tpu_custom_call" | custom-call | flops 2415919104 | bytes 5242880 | tf_op jit(solution)/shard_map/pallas_call | solution.py:434
  5.2 0.0 collective-permute-done.hubs_ref
  5.3 15.2 %all_to_all.21 = bf16[16,8,256]{2,1,0:T(8,128)(2,1)S(1)} all-to-all(bf16[16,8,256]{2,1,0:T(8,128)(2,1)S(1)} %bitcast.8), channel_id=1, replica_groups=mesh['dom'=8,'pair'=2,'side'=2] {'dom','pair'}, dimensions={0} | all-to-all | bytes 131072 | tf_op jit(solution)/shard_map/all_to_all | solution.py:379
  20.5 2.4 %shard_map.131 = (bf16[1024,256]{1,0:T(8,128)(2,1)}, f32[256,256]{1,0:T(8,128)S(1)}, f32[128,256]{1,0:T(8,128)S(1)}, bf16[384,256]{1,0:T(8,128)(2,1)S(1)}, bf16[...) custom-call(bf16[128,256]{1,0:T(8,128)(2,1)S(1)} %bitcast.7, ...), custom_call_target="tpu_custom_call" | custom-call | flops 671088640 | bytes 4194304 | tf_op jit(solution)/shard_map/pallas_call | solution.py:462
  22.9 0.1 collective-permute-start.1
  23.0 0.9 %shard_map.132.after_ref.feat_grad_ref = f32[1024,256]{1,0:T(8,128)S(1)} custom-call(bf16[1024,256]{1,0:T(8,128)(2,1)S(1)} %get-tuple-element.48.low_ref, bf16[256,256]{1,0:T(8,128)(2,1)S(1)} %get-tuple-element.34.w_self_ref, bf16[1024,1024]{1,0:T(8,128)(2,1)S(1)} %get-tuple-element.49.own_count_ref, bf16[1024,256]{1,0:T(8,128)(2,1)S(1)} %get-tuple-element.50.edge_grad_ref), custom_call_target="tpu_custom_call" | custom-call | flops 671088640 | bytes 2097152 | tf_op jit(solution)/shard_map/pallas_call | solution.py:485
  23.9 0.5 %collective-permute-done.1.received_ref = bf16[384,256]{1,0:T(8,128)(2,1)S(1)} collective-permute-done((bf16[384,256]{1,0:T(8,128)(2,1)S(1)}, bf16[384,256]{1,0:T(8,128)(2,1)S(1)}, u32[]{:S(2)}, u32[]{:S(2)}) %collective-permute-start.1) | collective-permute-done | bytes 196640 | tf_op jit(solution)/shard_map/ppermute | solution.py:383
  24.5 10.6 %all_to_all.22.slabs_ref = bf16[16,16,256]{2,1,0:T(8,128)(2,1)S(1)} all-to-all(bf16[16,16,256]{2,1,0:T(8,128)(2,1)S(1)} %shard_map.133), channel_id=1, replica_groups=mesh['dom'=8,'pair'=2,'side'=2] {'dom','pair'}, dimensions={0} | all-to-all | bytes 262144 | tf_op jit(solution)/shard_map/all_to_all | solution.py:379
  35.1 0.2 shard_map.134
  35.2 11.5 %all_to_all.23.message_ref.mine_ref = bf16[16,24,256]{2,1,0:T(8,128)(2,1)S(1)} all-to-all(bf16[16,24,256]{2,1,0:T(8,128)(2,1)S(1)} %shard_map.134), channel_id=1, replica_groups=mesh['dom'=8,'pair'=2,'side'=2] {'dom','pair'}, dimensions={0} | all-to-all | bytes 393216 | tf_op jit(solution)/shard_map/all_to_all | solution.py:379
  46.7 0.0 collective-permute-start.2
  46.7 1.2 %shard_map.135 = bf16[1024,256]{1,0:T(8,128)(2,1)} custom-call(bf16[16,24,256]{2,1,0:T(8,128)(2,1)S(1)} %all_to_all.23.message_ref.mine_ref, s32[1,128]{1,0:T(1,128)S(1)} %get-tuple-element.53.places_ref, f32[1024,256]{1,0:T(8,128)S(1)} %shard_map.132.after_ref.feat_grad_ref), custom_call_target="tpu_custom_call" | custom-call | flops 134217728 | bytes 1572864 | tf_op jit(solution)/shard_map/pallas_call | solution.py:500
  47.9 0.2 collective-permute-done.2.other_ref
  48.2 1.0 %shard_map.136 = (f32[256,256]{1,0:T(8,128)}, f32[256,256]{1,0:T(8,128)}, f32[1,256]{1,0:T(1,128)}) custom-call(bf16[16,24,256]{2,1,0:T(8,128)(2,1)S(1)} %all_to_all.23.message_ref.mine_ref, bf16[16,24,256]{2,1,0:T(8,128)(2,1)S(1)} %collective-permute-done.2.other_ref), custom_call_target="tpu_custom_call" | custom-call | tf_op jit(solution)/shard_map/pallas_call | solution.py:505
  (2 shorter events, 0.1 us)
Async XLA Ops:
  2.0 3.3 %collective-permute-start = (bf16[16,256]{1,0:T(8,128)(2,1)S(1)}, bf16[16,256]{1,0:T(8,128)(2,1)S(1)}, u32[]{:S(2)}, u32[]{:S(2)}) collective-permute-start(bf16[16,256]{1,0:T(8,128)(2,1)S(1)} %get-tuple-element.32), channel_id=1, source_target_pairs={{0,1},{1,0},{2,3},{3,2},{4,5},{5,4},{6,7},{7,6},{8,9},{9,8},{10,11... | collective-permute-start | bytes 24584 | tf_op jit(solution)/shard_map/ppermute | solution.py:383
  22.9 1.5 %collective-permute-start.1 = (bf16[384,256]{1,0:T(8,128)(2,1)S(1)}, bf16[384,256]{1,0:T(8,128)(2,1)S(1)}, u32[]{:S(2)}, u32[]{:S(2)}) collective-permute-start(bf16[384,256]{1,0:T(8,128)(2,1)S(1)} %get-tuple-element.47), channel_id=1, source_target_pairs={{0,1},{1,0},{2,3},{3,2},{4,5},{5,4},{6,7},{7,6},{8,9},{9,8},{10,11... | collective-permute-start | bytes 589832 | tf_op jit(solution)/shard_map/ppermute | solution.py:383
  46.7 1.4 %collective-permute-start.2 = (bf16[16,24,256]{2,1,0:T(8,128)(2,1)S(1)}, bf16[16,24,256]{2,1,0:T(8,128)(2,1)S(1)}, u32[]{:S(2)}, u32[]{:S(2)}) collective-permute-start(bf16[16,24,256]{2,1,0:T(8,128)(2,1)S(1)} %all_to_all.23.message_ref.mine_ref), channel_id=1, source_target_pairs={{0,1},{1,0},{2,3},{3,2},{4,5},{5,4},{6,7},{7,6},{8,9},{9,8},{10,11... | collective-permute-start | bytes 589832 | tf_op jit(solution)/shard_map/ppermute | solution.py:383
where the time goes:
time: 49.4 us; the launch traced here: 49.1 us
  blocking collectives  37.3 us (76%)
  Pallas kernels  9.75 us (20%)
  waiting for transfers between devices  0.78 us (2%)
  between operations  0.7 us (1%)
  starting transfers between devices  0.59 us (1%)
    all_to_all x3, blocking collectives, swap(): return lax.all_to_all(array, axes, split_axis=0, concat_axis=0, tiled=True)  37.3 us
    pallas_call x1, Pallas kernels, on_device(): call(functools.partial(own_kernel, sizes), (shape((width, width), BF16),...  2.75 us
    pallas_call x1, Pallas kernels, on_device(): call(functools.partial(joint_kernel, sizes), (pltpu.HBM((rows, width), BF...  2.41 us
    pallas_call x1, Pallas kernels, on_device(): call(functools.partial(pick_kernel, sizes), (shape((doms * tall, width),...  1.33 us
    pallas_call x1, Pallas kernels, on_device(): call(functools.partial(feat_grad_kernel, sizes, slab), shape((rows, width...  1.2 us
  transfers between devices with their start and end apart: 3, of which 2 were waited for; matrix products, arithmetic and copies ran while one was open for 0% of the time, Pallas kernels for 10%

commit v1 on v0

--- a/solution.py
+++ b/solution.py
@@ -175,6 +175,9 @@
 
     def own_sums(nodes):
         total_ref[:, nodes] = matmul(turned_ref[...], own_count_ref[:, nodes])
+
+    for first in range(0, rows, TILE):
+        nodes = slice(first, first + TILE)
         preact_ref[nodes, :] = matmul(feats_ref[nodes, :], w_self_ref[...]) + bias_ref[...]
 
     if rows + far_count_ref.shape[0] > 2048:
@@ -232,12 +235,22 @@
         mean_ref[:, nodes] = mean
         preact_ref[nodes, :] = self_ref[nodes, :] + matmul(mean, w_neigh_ref[...], 0, 0)
 
+    def node_sums(nodes):
+        low = low_ref[nodes, :]
+        return (
+            matmul(turned_ref[:, nodes], low),
+            matmul(mean_ref[:, nodes], low),
+            matmul(count_ref[:, nodes], edge_grad_ref[nodes, :]),
+        )
+
     bias_sum = jnp.zeros((8, width), F32)
     copies = []
     before_head(tiles[0])
     for number, nodes in enumerate(tiles):
         if number + 1 < len(tiles):
             before_head(tiles[number + 1])
+        elif number:
+            w_grad_ref[0], w_grad_ref[1], rest_ref[...] = node_sums(slice(0, nodes.start))
         for start in range(nodes.start, nodes.stop, PIECE):
             piece = slice(start, start + PIECE)
             preact = preact_ref[piece, :]
@@ -260,9 +273,13 @@
         edge_grad = matmul(low_ref[nodes, :], w_neigh_ref[...], 1, 1) * share_column
         edge_grad_ref[nodes, :] = edge_grad.astype(BF16)
 
-    w_grad_ref[0] = matmul(turned_ref[...], low_ref[...])
-    w_grad_ref[1] = matmul(mean_ref[...], low_ref[...])
-    remote = matmul(count_ref[...], edge_grad_ref[...])
+    w_self_sum, w_neigh_sum, remote = node_sums(tiles[-1])
+    if len(tiles) > 1:
+        w_self_sum = w_self_sum + w_grad_ref[0]
+        w_neigh_sum = w_neigh_sum + w_grad_ref[1]
+        remote = remote + rest_ref[...]
+    w_grad_ref[0] = w_self_sum
+    w_grad_ref[1] = w_neigh_sum
     rest_ref[...] = remote
     bias_ref[...] = bias_sum
     bias_sum = jnp.broadcast_to(jnp.sum(bias_sum, axis=0, keepdims=True), (tall, width))
@@ -345,18 +362,24 @@
         out_ref[nodes, :] = total.astype(BF16)
 
 
-def unit_kernel(slab, mine_ref, other_ref, unit_self_ref, unit_neigh_ref, unit_bias_ref, units_ref):
+def unit_kernel(slab, mine_ref, other_ref, self_hbm, neigh_hbm, unit_bias_ref, units_ref, sems):
     side = lax.axis_index("side")
-    size, width = unit_self_ref.shape
+    _, size, width = units_ref.shape
+    copies = [
+        pltpu.make_async_copy(units_ref.at[place], target, sems.at[place])
+        for place, target in enumerate((self_hbm, neigh_hbm))
+    ]
     for place, grad_ref in ((side, mine_ref), (1 - side, other_ref)):
         grad = grad_ref[: size // slab].astype(F32)[:, :slab, :].reshape(size, width)
         square = jnp.sum(jnp.sum(grad * grad, axis=0, keepdims=True), axis=1, keepdims=True)
         units_ref[place] = grad * lax.rsqrt(square * (1.0 / grad.size) + UNIT_EPS)
-    unit_self_ref[...] = units_ref[0]
-    unit_neigh_ref[...] = units_ref[1]
+        for number, copy in enumerate(copies):
+            pl.when(place == number)(copy.start)
     bias = jnp.sum(mine_ref[...].astype(F32)[:, slab:, :], axis=0)[-BIAS_ROWS:, :]
     bias = jnp.sum(bias, axis=0, keepdims=True)
     unit_bias_ref[...] = bias * lax.rsqrt(jnp.mean(bias * bias, axis=1, keepdims=True) + UNIT_EPS)
+    for copy in copies:
+        copy.wait()
 
 
 def call(kernel, out_shape, in_specs=None, scratch=(), cost=(0, 0), out_specs=None):
@@ -504,8 +527,9 @@
     )(message, places, feat_grad)
     unit_self, unit_neigh, unit_bias = call(
         functools.partial(unit_kernel, slab),
-        (shape((width, width), F32), shape((width, width), F32), shape((1, width), F32)),
-        scratch=(pltpu.VMEM((2, width, width), F32),),
+        (pltpu.HBM((width, width), F32), pltpu.HBM((width, width), F32), shape((1, width), F32)),
+        out_specs=(hbm, hbm, vmem),
+        scratch=(pltpu.VMEM((2, width, width), F32), pltpu.SemaphoreType.DMA((2,))),
     )(message, other_side(message))
     return outputs, grad_feats, unit_self, unit_neigh, unit_bias.reshape(width)
 

time: 49.4 us -> 49.9 us (1.010)
    pallas_call x1, Pallas kernels: 0.97 us -> 1.52 us  [on_device(): call(functools.partial(unit_kernel, slab), (pltpu.HBM((width, width), F32...]
where the time goes in v1:
time: 49.9 us; the launch traced here: 49.6 us
  blocking collectives  37.3 us (75%)
  Pallas kernels  10.2 us (20%)
  waiting for transfers between devices  0.78 us (2%)
  between operations  0.7 us (1%)
  starting transfers between devices  0.59 us (1%)
    all_to_all x3, blocking collectives, swap(): return lax.all_to_all(array, axes, split_axis=0, concat_axis=0, tiled=True)  37.3 us
    pallas_call x1, Pallas kernels, on_device(): call(functools.partial(own_kernel, sizes), (shape((width, width), BF16),...  2.8 us
    pallas_call x1, Pallas kernels, on_device(): call(functools.partial(joint_kernel, sizes), (pltpu.HBM((rows, width), BF...  2.28 us
    pallas_call x1, Pallas kernels, on_device(): call(functools.partial(unit_kernel, slab), (pltpu.HBM((width, width), F32...  1.52 us
    pallas_call x1, Pallas kernels, on_device(): call(functools.partial(pick_kernel, sizes), (shape((doms * tall, width),...  1.33 us
    pallas_call x1, Pallas kernels, on_device(): call(functools.partial(feat_grad_kernel, sizes, slab), shape((rows, width...  1.21 us
  transfers between devices with their start and end apart: 3, of which 2 were waited for; matrix products, arithmetic and copies ran while one was open for 0% of the time, Pallas kernels for 10%

profile of v1, /device:TPU:0, one launch (start us, length us, event | category | flops | bytes accessed | tf_op | source)
XLA Modules:
  0.0 49.6 jit_solution(3071316776529086956)
XLA Ops:
  0.6 1.3 %shard_map.128 = (bf16[64,256]{1,0:T(8,128)(2,1)S(1)}, bf16[16,256]{1,0:T(8,128)(2,1)S(1)}, s32[1,128]{1,0:T(1,128)S(1)}, bf16[1024,256]{1,0:T(8,128)(2,1)S(1)},...) custom-call(s32[2]{0:T(128)} %hub_hbm.1, ...), custom_call_target="tpu_custom_call" | custom-call | flops 67108864 | bytes 524288 | tf_op jit(solution)/shard_map/pallas_call | solution.py:426
  2.0 0.5 %collective-permute-start = (bf16[16,256]{1,0:T(8,128)(2,1)S(1)}, bf16[16,256]{1,0:T(8,128)(2,1)S(1)}, u32[]{:S(2)}, u32[]{:S(2)}) collective-permute-start(bf16[16,256]{1,0:T(8,128)(2,1)S(1)} %get-tuple-element.32), channel_id=1, source_target_pairs={{0,1},{1,0},{2,3},{3,2},{4,5},{5,4},{6,7},{7,6},{8,9},{9,8},{10,11... | collective-permute-start | bytes 24584 | tf_op jit(solution)/shard_map/ppermute | solution.py:406
  2.5 2.8 %shard_map.129 = (bf16[256,256]{1,0:T(8,128)(2,1)S(1)}, bf16[1024,256]{1,0:T(8,128)(2,1)S(1)}, f32[1,1024]{1,0:T(1,128)S(1)}, bf16[256,1024]{1,0:T(8,128)(2,1)S(...) custom-call(bf16[1024,256]{1,0:T(8,128)(2,1)S(1)} %get-tuple-element, ...), custom_call_target="tpu_custom_call" | custom-call | flops 2415919104 | bytes 5242880 | tf_op jit(solution)/shard_map/pallas_call | solution.py:457
  5.3 0.0 collective-permute-done.hubs_ref
  5.3 15.2 %all_to_all.21 = bf16[16,8,256]{2,1,0:T(8,128)(2,1)S(1)} all-to-all(bf16[16,8,256]{2,1,0:T(8,128)(2,1)S(1)} %bitcast.8), channel_id=1, replica_groups=mesh['dom'=8,'pair'=2,'side'=2] {'dom','pair'}, dimensions={0} | all-to-all | bytes 131072 | tf_op jit(solution)/shard_map/all_to_all | solution.py:402
  20.6 2.3 %shard_map.131 = (bf16[1024,256]{1,0:T(8,128)(2,1)}, f32[256,256]{1,0:T(8,128)S(1)}, f32[128,256]{1,0:T(8,128)S(1)}, bf16[384,256]{1,0:T(8,128)(2,1)S(1)}, bf16[...) custom-call(bf16[128,256]{1,0:T(8,128)(2,1)S(1)} %bitcast.7, ...), custom_call_target="tpu_custom_call" | custom-call | flops 671088640 | bytes 4194304 | tf_op jit(solution)/shard_map/pallas_call | solution.py:485
  22.8 0.1 collective-permute-start.1
  22.9 0.9 %shard_map.132.after_ref.feat_grad_ref = f32[1024,256]{1,0:T(8,128)S(1)} custom-call(bf16[1024,256]{1,0:T(8,128)(2,1)S(1)} %get-tuple-element.48.low_ref, bf16[256,256]{1,0:T(8,128)(2,1)S(1)} %get-tuple-element.34.w_self_ref, bf16[1024,1024]{1,0:T(8,128)(2,1)S(1)} %get-tuple-element.49.own_count_ref, bf16[1024,256]{1,0:T(8,128)(2,1)S(1)} %get-tuple-element.50.edge_grad_ref), custom_call_target="tpu_custom_call" | custom-call | flops 671088640 | bytes 2097152 | tf_op jit(solution)/shard_map/pallas_call | solution.py:508
  23.8 0.5 %collective-permute-done.1.received_ref = bf16[384,256]{1,0:T(8,128)(2,1)S(1)} collective-permute-done((bf16[384,256]{1,0:T(8,128)(2,1)S(1)}, bf16[384,256]{1,0:T(8,128)(2,1)S(1)}, u32[]{:S(2)}, u32[]{:S(2)}) %collective-permute-start.1) | collective-permute-done | bytes 196640 | tf_op jit(solution)/shard_map/ppermute | solution.py:406
  24.4 10.6 %all_to_all.22.slabs_ref = bf16[16,16,256]{2,1,0:T(8,128)(2,1)S(1)} all-to-all(bf16[16,16,256]{2,1,0:T(8,128)(2,1)S(1)} %shard_map.133), channel_id=1, replica_groups=mesh['dom'=8,'pair'=2,'side'=2] {'dom','pair'}, dimensions={0} | all-to-all | bytes 262144 | tf_op jit(solution)/shard_map/all_to_all | solution.py:402
  35.0 0.2 shard_map.134
  35.2 11.5 %all_to_all.23.message_ref.mine_ref = bf16[16,24,256]{2,1,0:T(8,128)(2,1)S(1)} all-to-all(bf16[16,24,256]{2,1,0:T(8,128)(2,1)S(1)} %shard_map.134), channel_id=1, replica_groups=mesh['dom'=8,'pair'=2,'side'=2] {'dom','pair'}, dimensions={0} | all-to-all | bytes 393216 | tf_op jit(solution)/shard_map/all_to_all | solution.py:402
  46.7 0.0 collective-permute-start.2
  46.7 1.2 %shard_map.135 = bf16[1024,256]{1,0:T(8,128)(2,1)} custom-call(bf16[16,24,256]{2,1,0:T(8,128)(2,1)S(1)} %all_to_all.23.message_ref.mine_ref, s32[1,128]{1,0:T(1,128)S(1)} %get-tuple-element.53.places_ref, f32[1024,256]{1,0:T(8,128)S(1)} %shard_map.132.after_ref.feat_grad_ref), custom_call_target="tpu_custom_call" | custom-call | flops 134217728 | bytes 1572864 | tf_op jit(solution)/shard_map/pallas_call | solution.py:523
  47.9 0.2 collective-permute-done.2.other_ref
  48.1 1.5 %shard_map.136 = (f32[256,256]{1,0:T(8,128)}, f32[256,256]{1,0:T(8,128)}, f32[1,256]{1,0:T(1,128)}) custom-call(bf16[16,24,256]{2,1,0:T(8,128)(2,1)S(1)} %all_to_all.23.message_ref.mine_ref, bf16[16,24,256]{2,1,0:T(8,128)(2,1)S(1)} %collective-permute-done.2.other_ref), custom_call_target="tpu_custom_call" | custom-call | tf_op jit(solution)/shard_map/pallas_call | solution.py:528
  (2 shorter events, 0.1 us)
Async XLA Ops:
  2.0 3.3 %collective-permute-start = (bf16[16,256]{1,0:T(8,128)(2,1)S(1)}, bf16[16,256]{1,0:T(8,128)(2,1)S(1)}, u32[]{:S(2)}, u32[]{:S(2)}) collective-permute-start(bf16[16,256]{1,0:T(8,128)(2,1)S(1)} %get-tuple-element.32), channel_id=1, source_target_pairs={{0,1},{1,0},{2,3},{3,2},{4,5},{5,4},{6,7},{7,6},{8,9},{9,8},{10,11... | collective-permute-start | bytes 24584 | tf_op jit(solution)/shard_map/ppermute | solution.py:406
  22.8 1.5 %collective-permute-start.1 = (bf16[384,256]{1,0:T(8,128)(2,1)S(1)}, bf16[384,256]{1,0:T(8,128)(2,1)S(1)}, u32[]{:S(2)}, u32[]{:S(2)}) collective-permute-start(bf16[384,256]{1,0:T(8,128)(2,1)S(1)} %get-tuple-element.47), channel_id=1, source_target_pairs={{0,1},{1,0},{2,3},{3,2},{4,5},{5,4},{6,7},{7,6},{8,9},{9,8},{10,11... | collective-permute-start | bytes 589832 | tf_op jit(solution)/shard_map/ppermute | solution.py:406
  46.7 1.4 %collective-permute-start.2 = (bf16[16,24,256]{2,1,0:T(8,128)(2,1)S(1)}, bf16[16,24,256]{2,1,0:T(8,128)(2,1)S(1)}, u32[]{:S(2)}, u32[]{:S(2)}) collective-permute-start(bf16[16,24,256]{2,1,0:T(8,128)(2,1)S(1)} %all_to_all.23.message_ref.mine_ref), channel_id=1, source_target_pairs={{0,1},{1,0},{2,3},{3,2},{4,5},{5,4},{6,7},{7,6},{8,9},{9,8},{10,11... | collective-permute-start | bytes 589832 | tf_op jit(solution)/shard_map/ppermute | solution.py:406

commit v2 on v1

--- a/solution.py
+++ b/solution.py
@@ -60,14 +60,12 @@
 
 def pick_kernel(sizes, hub_hbm, send_hbm, *refs):
     doms, reps, cap, hub_own, tall = sizes
-    inputs, (rows_ref, hubs_ref, places_ref), kept, (hub_ref, send_ref, sems) = (
-        refs[:5],
-        refs[5:8],
-        refs[8:13],
-        refs[13:],
-    )
+    inputs, (rows_ref, hubs_ref, places_ref), refs = refs[:5], refs[5:8], refs[8:]
+    kept, (slot_ref, share_ref, own_count_ref, far_count_ref), refs = refs[:3], refs[3:7], refs[7:]
+    hub_ref, send_ref, degree_ref, edge_ref, hot_ref, sems = refs
     feats_ref = kept[0]
-    copies = fetch(((hub_hbm, hub_ref), (send_hbm, send_ref), *zip(inputs, kept)), sems)
+    targets = (hub_ref, send_ref, degree_ref, edge_ref, *kept)
+    copies = fetch(zip((hub_hbm, send_hbm, *inputs), targets), sems)
     slots = doms * tall
     lane = iota(places_ref.shape, 1)
     row = remainder(lane, tall)
@@ -96,10 +94,14 @@
         for first in range(0, feats_ref.shape[0], LANES)
     ]
     copies[2].wait()
+    copies[3].wait()
+    find_slots(sizes, degree_ref, edge_ref, slot_ref, share_ref)
+    count_edges(slot_ref, own_count_ref, far_count_ref, hot_ref, slice(0, TILE))
+    copies[4].wait()
     picked = matmul(jnp.concatenate(chosen, axis=1), feats_ref[...]).astype(BF16)
     rows_ref[...] = picked[:slots, :]
     hubs_ref[...] = picked[slots:, :]
-    for copy in copies[3:]:
+    for copy in copies[5:]:
         copy.wait()
 
 
@@ -135,30 +137,33 @@
     for strip in range(0, LANES, STRIP):
         numbers = (iota((STRIP, TILE), 0) + strip).astype(jnp.int16)
         hot = [jnp.where(numbers == low[k], BF16(1.0), BF16(0.0)) for k in range(fanout)]
-        for block in range(highs):
-            count = hot[0] * hot_ref[block * fanout]
+
+        def count(block):
+            total = hot[0] * hot_ref[block * fanout]
             for k in range(1, fanout):
-                count = count + hot[k] * hot_ref[block * fanout + k]
+                total = total + hot[k] * hot_ref[block * fanout + k]
+            return total
+
+        for block in range(rows // LANES):
             first = block * LANES + strip
-            if first < rows:
-                own_count_ref[first : first + STRIP, nodes] = count
-            else:
-                far_count_ref[first - rows : first - rows + STRIP, nodes] = count
-
-
-def own_kernel(sizes, feats_ref, w_self_ref, bias_ref, degree_ref, edge_ref, *refs):
+            own_count_ref[first : first + STRIP, :] = count(block)
+        far = far_count_ref.shape[0] // LANES
+        if far <= 4:
+            for block in range(far):
+                first = block * LANES + strip
+                far_count_ref[first : first + STRIP, :] = count(rows // LANES + block)
+        else:
+
+            @pl.loop(0, far)
+            def far_block(block):
+                first = pl.multiple_of(block * LANES + strip, STRIP)
+                far_count_ref[pl.ds(first, STRIP), :] = count(rows // LANES + block)
+
+
+def find_slots(sizes, degree_ref, edge_ref, slot_ref, share_ref):
     doms, reps, cap, hub_own, tall = sizes
-    inputs, refs = refs[:2], refs[2:]
-    kept, (share_ref, turned_ref, own_count_ref, far_count_ref, total_ref, preact_ref) = (
-        refs[:2],
-        refs[2:8],
-    )
-    slot_ref, hot_ref, sems = refs[8:]
-    copies = fetch(zip(inputs, kept), sems)
-    rows = feats_ref.shape[0]
-    fanout = edge_ref.shape[0]
+    fanout, rows = edge_ref.shape
     hubs = doms * reps * hub_own
-
     source = edge_ref[...]
     hub = source - rows
     halo = hub - hubs
@@ -171,86 +176,84 @@
     valid = jnp.minimum(degree_ref[...], fanout)
     slot_ref[...] = jnp.where(iota((fanout, rows), 0) < valid, slot, -1)
     share_ref[...] = 1.0 / valid.astype(F32)
+
+
+def own_kernel(tiles, feats_ref, w_self_ref, bias_ref, slot_ref, *refs):
+    first_count_ref, inputs, kept, refs = refs[0], refs[1:3], refs[3:5], refs[5:]
+    turned_ref, total_ref, preact_ref = refs[:3]
+    own_refs, far_refs, (hot_ref, sems) = (
+        refs[3 : 2 + tiles],
+        refs[2 + tiles : 1 + 2 * tiles],
+        refs[1 + 2 * tiles :],
+    )
+    copies = fetch(zip(inputs, kept), sems)
     turned_ref[...] = feats_ref[...].T
 
-    def own_sums(nodes):
-        total_ref[:, nodes] = matmul(turned_ref[...], own_count_ref[:, nodes])
-
-    for first in range(0, rows, TILE):
-        nodes = slice(first, first + TILE)
+    def own_sums(number, count_ref):
+        nodes = slice(number * TILE, (number + 1) * TILE)
+        total_ref[:, nodes] = matmul(turned_ref[...], count_ref[...])
         preact_ref[nodes, :] = matmul(feats_ref[nodes, :], w_self_ref[...]) + bias_ref[...]
 
-    if rows + far_count_ref.shape[0] > 2048:
-
-        @pl.loop(0, rows, step=TILE)
-        def node_tile(first):
-            nodes = pl.ds(pl.multiple_of(first, TILE), TILE)
-            count_edges(slot_ref, own_count_ref, far_count_ref, hot_ref.at[0], nodes)
-            own_sums(nodes)
-
-    else:
-        counted = None
-        for number in range(rows // TILE):
-            nodes = slice(number * TILE, (number + 1) * TILE)
-            count_edges(slot_ref, own_count_ref, far_count_ref, hot_ref.at[number % 2], nodes)
-            if counted is not None:
-                own_sums(counted)
-            counted = nodes
-        own_sums(counted)
+    counted = first_count_ref
+    for number in range(1, tiles):
+        nodes = slice(number * TILE, (number + 1) * TILE)
+        own_ref, far_ref = own_refs[number - 1], far_refs[number - 1]
+        count_edges(slot_ref, own_ref, far_ref, hot_ref.at[number % 2], nodes)
+        own_sums(number - 1, counted)
+        counted = own_ref
+    own_sums(tiles - 1, counted)
     for copy in copies:
         copy.wait()
 
 
-def joint_kernel(
-    sizes,
-    remote_ref,
-    turned_ref,
-    total_ref,
-    self_ref,
-    count_ref,
-    share_ref,
-    w_neigh_ref,
-    cot_ref,
-    outputs_hbm,
-    w_own_ref,
-    rest_ref,
-    message_ref,
-    low_ref,
-    edge_grad_ref,
-    bias_ref,
-    outputs_ref,
-    mean_ref,
-    preact_ref,
-    w_grad_ref,
-    sems,
-):
+def joint_kernel(sizes, remote_ref, turned_ref, total_ref, self_ref, *refs):
     doms, reps, cap, hub_own, tall = sizes
-    rows, width = outputs_ref.shape
+    rows, width = self_ref.shape
     tiles = [slice(first, first + TILE) for first in range(0, rows, TILE)]
+    count_refs, refs = refs[: len(tiles)], refs[len(tiles) :]
+    (
+        share_ref,
+        w_neigh_ref,
+        cot_ref,
+        outputs_hbm,
+        w_own_ref,
+        rest_ref,
+        message_ref,
+        low_ref,
+        edge_grad_ref,
+        bias_ref,
+        outputs_ref,
+        mean_ref,
+        preact_ref,
+        w_grad_ref,
+        sems,
+    ) = refs
     table = remote_ref[...].T
 
-    def before_head(nodes):
-        mean = total_ref[:, nodes] + matmul(table, count_ref[:, nodes])
+    def before_head(number):
+        nodes = tiles[number]
+        mean = total_ref[:, nodes] + matmul(table, count_refs[number][...])
         mean = (mean * share_ref[:, nodes]).astype(BF16)
         mean_ref[:, nodes] = mean
         preact_ref[nodes, :] = self_ref[nodes, :] + matmul(mean, w_neigh_ref[...], 0, 0)
 
-    def node_sums(nodes):
+    def node_sums(numbers):
+        nodes = slice(tiles[numbers[0]].start, tiles[numbers[-1]].stop)
         low = low_ref[nodes, :]
         return (
             matmul(turned_ref[:, nodes], low),
             matmul(mean_ref[:, nodes], low),
-            matmul(count_ref[:, nodes], edge_grad_ref[nodes, :]),
+            sum(matmul(count_refs[k][...], edge_grad_ref[tiles[k], :]) for k in numbers),
         )
 
     bias_sum = jnp.zeros((8, width), F32)
     copies = []
-    before_head(tiles[0])
+    before_head(0)
     for number, nodes in enumerate(tiles):
         if number + 1 < len(tiles):
-            before_head(tiles[number + 1])
+            before_head(number + 1)
         elif number:
-            w_grad_ref[0], w_grad_ref[1], rest_ref[...] = node_sums(slice(0, nodes.start))
+            w_grad_ref[0], w_grad_ref[1], rest_ref[...] = node_sums(range(number))
         for start in range(nodes.start, nodes.stop, PIECE):
             piece = slice(start, start + PIECE)
             preact = preact_ref[piece, :]
@@ -273,7 +276,7 @@
         edge_grad = matmul(low_ref[nodes, :], w_neigh_ref[...], 1, 1) * share_column
         edge_grad_ref[nodes, :] = edge_grad.astype(BF16)
 
-    w_self_sum, w_neigh_sum, remote = node_sums(tiles[-1])
+    w_self_sum, w_neigh_sum, remote = node_sums([len(tiles) - 1])
     if len(tiles) > 1:
         w_self_sum = w_self_sum + w_grad_ref[0]
         w_neigh_sum = w_neigh_sum + w_grad_ref[1]
@@ -297,12 +300,15 @@
         copy.wait()
 
 
-def own_grad_kernel(low_ref, w_self_ref, own_count_ref, edge_grad_ref, feat_grad_ref):
+def own_grad_kernel(low_ref, w_self_ref, edge_grad_ref, *refs):
+    *count_refs, feat_grad_ref = refs
     for first in range(0, low_ref.shape[0], TILE):
         nodes = slice(first, first + TILE)
-        feat_grad_ref[nodes, :] = matmul(own_count_ref[nodes, :], edge_grad_ref[...]) + matmul(
-            low_ref[nodes, :], w_self_ref[...], 1, 1
-        )
+        total = matmul(low_ref[nodes, :], w_self_ref[...], 1, 1)
+        for number, count_ref in enumerate(count_refs):
+            edges = edge_grad_ref[number * TILE : (number + 1) * TILE, :]
+            total = total + matmul(count_ref[nodes, :], edges)
+        feat_grad_ref[nodes, :] = total
 
 
 def side_sum_kernel(own_ref, received_ref, after_ref, message_ref):
@@ -362,22 +368,25 @@
         out_ref[nodes, :] = total.astype(BF16)
 
 
-def unit_kernel(slab, mine_ref, other_ref, self_hbm, neigh_hbm, unit_bias_ref, units_ref, sems):
+def unit_kernel(slab, mine_ref, other_ref, self_hbm, neigh_hbm, bias_hbm, units_ref, bias_ref, sems):
     side = lax.axis_index("side")
     _, size, width = units_ref.shape
+    bias = jnp.sum(mine_ref[...].astype(F32)[:, slab:, :], axis=0)[-BIAS_ROWS:, :]
+    bias = jnp.sum(bias, axis=0, keepdims=True)
+    bias_ref[...] = bias * lax.rsqrt(jnp.mean(bias * bias, axis=1, keepdims=True) + UNIT_EPS)
     copies = [
-        pltpu.make_async_copy(units_ref.at[place], target, sems.at[place])
-        for place, target in enumerate((self_hbm, neigh_hbm))
+        pltpu.make_async_copy(source, target, sems.at[number])
+        for number, (source, target) in enumerate(
+            ((units_ref.at[0], self_hbm), (units_ref.at[1], neigh_hbm), (bias_ref, bias_hbm))
+        )
     ]
+    copies[2].start()
     for place, grad_ref in ((side, mine_ref), (1 - side, other_ref)):
         grad = grad_ref[: size // slab].astype(F32)[:, :slab, :].reshape(size, width)
         square = jnp.sum(jnp.sum(grad * grad, axis=0, keepdims=True), axis=1, keepdims=True)
         units_ref[place] = grad * lax.rsqrt(square * (1.0 / grad.size) + UNIT_EPS)
-        for number, copy in enumerate(copies):
+        for number, copy in enumerate(copies[:2]):
             pl.when(place == number)(copy.start)
-    bias = jnp.sum(mine_ref[...].astype(F32)[:, slab:, :], axis=0)[-BIAS_ROWS:, :]
-    bias = jnp.sum(bias, axis=0, keepdims=True)
-    unit_bias_ref[...] = bias * lax.rsqrt(jnp.mean(bias * bias, axis=1, keepdims=True) + UNIT_EPS)
     for copy in copies:
         copy.wait()
 
@@ -423,7 +432,9 @@
     hbm = pl.BlockSpec(memory_space=pltpu.HBM)
     vmem = pl.BlockSpec(memory_space=pltpu.VMEM)
 
-    picked, hubs, places, *kept = call(
+    tiles = rows // TILE
+    hot = pltpu.VMEM(((rows + slots) // LANES * fanout, STRIP, TILE), BF16)
+    picked, hubs, places, feats_kept, w_self_kept, bias_kept, slot, share, *first_counts = call(
         functools.partial(pick_kernel, sizes),
         (
             shape((doms * tall, width), BF16),
@@ -432,13 +443,18 @@
             shape((rows, width), BF16),
             shape((width, width), BF16),
             shape((1, width), F32),
-            shape((1, rows), jnp.int32),
             shape((fanout, rows), jnp.int32),
+            shape((1, rows), F32),
+            shape((rows, TILE), BF16),
+            shape((slots, TILE), BF16),
         ),
         [hbm] * 7,
         (
             pltpu.SMEM((hub_own,), jnp.int32),
             pltpu.SMEM((cap, doms), jnp.int32),
+            pltpu.VMEM((1, rows), jnp.int32),
+            pltpu.VMEM((fanout, rows), jnp.int32),
+            hot,
             pltpu.SemaphoreType.DMA((7,)),
         ),
         cost=(2 * rows * slots * width, 2 * rows * width),
@@ -446,40 +462,39 @@
         *in_hbm(
             hub_rows,
             send_rows.T,
+            degree.reshape(1, rows),
+            edge_src.T,
             feats,
             w_self,
             bias.reshape(1, width),
-            degree.reshape(1, rows),
-            edge_src.T,
         )
     )
     hubs = other_side(hubs)
-    w_neigh_kept, cot_kept, share, turned, own_count, far_count, own_total, self_part = call(
-        functools.partial(own_kernel, sizes),
+    w_neigh_kept, cot_kept, turned, own_total, self_part, *counts = call(
+        functools.partial(own_kernel, tiles),
         (
             shape((width, width), BF16),
             shape((rows, width), BF16),
-            shape((1, rows), F32),
             shape((width, rows), BF16),
-            shape((rows, rows), BF16),
-            shape((slots, rows), BF16),
             shape((width, rows), F32),
             shape((rows, width), F32),
+            *((shape((rows, TILE), BF16),) * (tiles - 1)),
+            *((shape((slots, TILE), BF16),) * (tiles - 1)),
         ),
         [vmem] * 5 + [hbm] * 2,
         (
-            pltpu.VMEM((fanout, rows), jnp.int32),
-            pltpu.VMEM((2, (rows + slots) // LANES * fanout, STRIP, TILE), BF16),
+            pltpu.VMEM((2, *hot.shape), BF16),
             pltpu.SemaphoreType.DMA((2,)),
         ),
         cost=(8 * rows * (rows + slots) * width, 12 * rows * width + 2 * rows * rows),
-    )(*kept, *in_hbm(w_neigh, out_cot))
-
+    )(feats_kept, w_self_kept, bias_kept, slot, first_counts[0], *in_hbm(w_neigh, out_cot))
+    own_counts = [first_counts[0], *counts[: tiles - 1]]
+    far_counts = [first_counts[1], *counts[tiles - 1 :]]
     message = call(
         functools.partial(message_kernel, sizes),
         shape((slots, width), BF16),
         [vmem, vmem, pl.BlockSpec(memory_space=pl.ANY)],
-    )(picked, hubs, share)
+    )(picked, hubs, own_total)
     remote = swap(message, PEERS)
 
     outputs, w_own, rest, message, low, edge_grad, bias_sum = call(
@@ -502,14 +517,14 @@
             pltpu.SemaphoreType.DMA((rows // TILE,)),
         ),
         cost=(4 * rows * slots * width + 8 * rows * width * width, 16 * rows * width),
-    )(remote, turned, own_total, self_part, far_count, share, w_neigh_kept, cot_kept)
+    )(remote, turned, own_total, self_part, *far_counts, share, w_neigh_kept, cot_kept)
 
     received = other_side(message)
     feat_grad = call(
         own_grad_kernel,
         shape((rows, width), F32),
         cost=(2 * rows * rows * width + 2 * rows * width * width, 8 * rows * width),
-    )(low, kept[1], own_count, edge_grad)
+    )(low, w_self_kept, edge_grad, *own_counts)
     message = call(
         side_sum_kernel,
         shape((peers, slab, width), BF16),
@@ -527,9 +542,13 @@
     )(message, places, feat_grad)
     unit_self, unit_neigh, unit_bias = call(
         functools.partial(unit_kernel, slab),
-        (pltpu.HBM((width, width), F32), pltpu.HBM((width, width), F32), shape((1, width), F32)),
-        out_specs=(hbm, hbm, vmem),
-        scratch=(pltpu.VMEM((2, width, width), F32), pltpu.SemaphoreType.DMA((2,))),
+        (*((pltpu.HBM((width, width), F32),) * 2), pltpu.HBM((1, width), F32)),
+        out_specs=(hbm,) * 3,
+        scratch=(
+            pltpu.VMEM((2, width, width), F32),
+            pltpu.VMEM((1, width), F32),
+            pltpu.SemaphoreType.DMA((3,)),
+        ),
     )(message, other_side(message))
     return outputs, grad_feats, unit_self, unit_neigh, unit_bias.reshape(width)
 

time: 49.9 us -> 49.3 us (0.988)
  Pallas kernels: 10.2 us -> 9.56 us
    pallas_call x2, Pallas kernels: 4.32 us -> 3.18 us  [the longest x1 2.2 us: on_device(): call(functools.partial(own_kernel, tiles), (shape((width, width), BF16),...]
  transfers between devices with their start and end apart: 3 -> 3, of which waited for: 2 -> 2; matrix products, arithmetic and copies ran while one was open for 0% -> 0% of each run, Pallas kernels for 10% -> 9%
where the time goes in v2:
time: 49.3 us; the launch traced here: 49 us
  blocking collectives  37.3 us (76%)
  Pallas kernels  9.56 us (19%)
  waiting for transfers between devices  0.81 us (2%)
  between operations  0.7 us (1%)
  starting transfers between devices  0.59 us (1%)
    all_to_all x3, blocking collectives, swap(): return lax.all_to_all(array, axes, split_axis=0, concat_axis=0, tiled=True)  37.3 us
    pallas_call x1, Pallas kernels, on_device(): call(functools.partial(joint_kernel, sizes), (pltpu.HBM((rows, width), BF...  2.37 us
    pallas_call x1, Pallas kernels, on_device(): call(functools.partial(own_kernel, tiles), (shape((width, width), BF16),...  2.2 us
    pallas_call x1, Pallas kernels, on_device(): call(functools.partial(pick_kernel, sizes), (shape((doms * tall, width),...  1.75 us
    pallas_call x1, Pallas kernels, on_device(): call(functools.partial(feat_grad_kernel, sizes, slab), shape((rows, width...  1.2 us
  transfers between devices with their start and end apart: 3, of which 2 were waited for; matrix products, arithmetic and copies ran while one was open for 0% of the time, Pallas kernels for 9%

profile of v2, /device:TPU:0, one launch (start us, length us, event | category | flops | bytes accessed | tf_op | source)
XLA Modules:
  0.0 49.0 jit_solution(16811848743642202366)
XLA Ops:
  0.6 1.8 %shard_map.128 = (bf16[64,256]{1,0:T(8,128)(2,1)S(1)}, bf16[16,256]{1,0:T(8,128)(2,1)S(1)}, s32[1,128]{1,0:T(1,128)S(1)}, bf16[1024,256]{1,0:T(8,128)(2,1)S(1)},...) custom-call(s32[2]{0:T(128)} %hub_hbm.1, ...), custom_call_target="tpu_custom_call" | custom-call | flops 67108864 | bytes 524288 | tf_op jit(solution)/shard_map/pallas_call | solution.py:437
  2.4 0.5 %collective-permute-start = (bf16[16,256]{1,0:T(8,128)(2,1)S(1)}, bf16[16,256]{1,0:T(8,128)(2,1)S(1)}, u32[]{:S(2)}, u32[]{:S(2)}) collective-permute-start(bf16[16,256]{1,0:T(8,128)(2,1)S(1)} %get-tuple-element.37), channel_id=1, source_target_pairs={{0,1},{1,0},{2,3},{3,2},{4,5},{5,4},{6,7},{7,6},{8,9},{9,8},{10,11... | collective-permute-start | bytes 24584 | tf_op jit(solution)/shard_map/ppermute | solution.py:415
  2.9 2.2 %shard_map.129 = (bf16[256,256]{1,0:T(8,128)(2,1)S(1)}, bf16[1024,256]{1,0:T(8,128)(2,1)S(1)}, bf16[256,1024]{1,0:T(8,128)(2,1)S(1)}, f32[256,1024]{1,0:T(8,128)...) custom-call(bf16[1024,256]{1,0:T(8,128)(2,1)S(1)} %get-tuple-element, ...), custom_call_target="tpu_custom_call" | custom-call | flops 2415919104 | bytes 5242880 | tf_op jit(solution)/shard_map/pallas_call | solution.py:473
  5.1 0.0 collective-permute-done.hubs_ref
  5.2 15.2 %all_to_all.21 = bf16[16,8,256]{2,1,0:T(8,128)(2,1)S(1)} all-to-all(bf16[16,8,256]{2,1,0:T(8,128)(2,1)S(1)} %bitcast.8), channel_id=1, replica_groups=mesh['dom'=8,'pair'=2,'side'=2] {'dom','pair'}, dimensions={0} | all-to-all | bytes 131072 | tf_op jit(solution)/shard_map/all_to_all | solution.py:411
  20.4 2.4 %shard_map.131 = (bf16[1024,256]{1,0:T(8,128)(2,1)}, f32[256,256]{1,0:T(8,128)S(1)}, f32[128,256]{1,0:T(8,128)S(1)}, bf16[384,256]{1,0:T(8,128)(2,1)S(1)}, bf16[...) custom-call(bf16[128,256]{1,0:T(8,128)(2,1)S(1)} %bitcast.7, ...), custom_call_target="tpu_custom_call" | custom-call | flops 671088640 | bytes 4194304 | tf_op jit(solution)/shard_map/pallas_call | solution.py:500
  22.8 0.1 collective-permute-start.1
  22.8 0.8 %shard_map.132.after_ref.feat_grad_ref = f32[1024,256]{1,0:T(8,128)S(1)} custom-call(bf16[1024,256]{1,0:T(8,128)(2,1)S(1)} %get-tuple-element.56.low_ref, bf16[256,256]{1,0:T(8,128)(2,1)S(1)} %get-tuple-element.39.w_self_ref, bf16[1024,256]{1,0:T(8,128)(2,1)S(1)} %get-tuple-element.57.edge_grad_ref, bf16[1024,256]{1,0:T(8,128)(2,1)S(1)} %get-tuple-element.42.refs_0_, ...), custom_call_target="tpu_custom_call" | custom-call | flops 671088640 | bytes 2097152 | tf_op jit(solution)/shard_map/pallas_call | solution.py:523
  23.7 0.6 %collective-permute-done.1.received_ref = bf16[384,256]{1,0:T(8,128)(2,1)S(1)} collective-permute-done((bf16[384,256]{1,0:T(8,128)(2,1)S(1)}, bf16[384,256]{1,0:T(8,128)(2,1)S(1)}, u32[]{:S(2)}, u32[]{:S(2)}) %collective-permute-start.1) | collective-permute-done | bytes 196640 | tf_op jit(solution)/shard_map/ppermute | solution.py:415
  24.3 10.6 %all_to_all.22.slabs_ref = bf16[16,16,256]{2,1,0:T(8,128)(2,1)S(1)} all-to-all(bf16[16,16,256]{2,1,0:T(8,128)(2,1)S(1)} %shard_map.133), channel_id=1, replica_groups=mesh['dom'=8,'pair'=2,'side'=2] {'dom','pair'}, dimensions={0} | all-to-all | bytes 262144 | tf_op jit(solution)/shard_map/all_to_all | solution.py:411
  34.9 0.2 shard_map.134
  35.1 11.5 %all_to_all.23.message_ref.mine_ref = bf16[16,24,256]{2,1,0:T(8,128)(2,1)S(1)} all-to-all(bf16[16,24,256]{2,1,0:T(8,128)(2,1)S(1)} %shard_map.134), channel_id=1, replica_groups=mesh['dom'=8,'pair'=2,'side'=2] {'dom','pair'}, dimensions={0} | all-to-all | bytes 393216 | tf_op jit(solution)/shard_map/all_to_all | solution.py:411
  46.6 0.0 collective-permute-start.2
  46.6 1.2 %shard_map.135 = bf16[1024,256]{1,0:T(8,128)(2,1)} custom-call(bf16[16,24,256]{2,1,0:T(8,128)(2,1)S(1)} %all_to_all.23.message_ref.mine_ref, s32[1,128]{1,0:T(1,128)S(1)} %get-tuple-element.63.places_ref, f32[1024,256]{1,0:T(8,128)S(1)} %shard_map.132.after_ref.feat_grad_ref), custom_call_target="tpu_custom_call" | custom-call | flops 134217728 | bytes 1572864 | tf_op jit(solution)/shard_map/pallas_call | solution.py:538
  47.8 0.2 collective-permute-done.2.other_ref
  48.0 1.0 %shard_map.136 = (f32[256,256]{1,0:T(8,128)}, f32[256,256]{1,0:T(8,128)}, f32[1,256]{1,0:T(1,128)}) custom-call(bf16[16,24,256]{2,1,0:T(8,128)(2,1)S(1)} %all_to_all.23.message_ref.mine_ref, bf16[16,24,256]{2,1,0:T(8,128)(2,1)S(1)} %collective-permute-done.2.other_ref), custom_call_target="tpu_custom_call" | custom-call | tf_op jit(solution)/shard_map/pallas_call | solution.py:543
  (2 shorter events, 0.1 us)
Async XLA Ops:
  2.4 2.7 %collective-permute-start = (bf16[16,256]{1,0:T(8,128)(2,1)S(1)}, bf16[16,256]{1,0:T(8,128)(2,1)S(1)}, u32[]{:S(2)}, u32[]{:S(2)}) collective-permute-start(bf16[16,256]{1,0:T(8,128)(2,1)S(1)} %get-tuple-element.37), channel_id=1, source_target_pairs={{0,1},{1,0},{2,3},{3,2},{4,5},{5,4},{6,7},{7,6},{8,9},{9,8},{10,11... | collective-permute-start | bytes 24584 | tf_op jit(solution)/shard_map/ppermute | solution.py:415
  22.8 1.5 %collective-permute-start.1 = (bf16[384,256]{1,0:T(8,128)(2,1)S(1)}, bf16[384,256]{1,0:T(8,128)(2,1)S(1)}, u32[]{:S(2)}, u32[]{:S(2)}) collective-permute-start(bf16[384,256]{1,0:T(8,128)(2,1)S(1)} %get-tuple-element.55), channel_id=1, source_target_pairs={{0,1},{1,0},{2,3},{3,2},{4,5},{5,4},{6,7},{7,6},{8,9},{9,8},{10,11... | collective-permute-start | bytes 589832 | tf_op jit(solution)/shard_map/ppermute | solution.py:415
  46.6 1.4 %collective-permute-start.2 = (bf16[16,24,256]{2,1,0:T(8,128)(2,1)S(1)}, bf16[16,24,256]{2,1,0:T(8,128)(2,1)S(1)}, u32[]{:S(2)}, u32[]{:S(2)}) collective-permute-start(bf16[16,24,256]{2,1,0:T(8,128)(2,1)S(1)} %all_to_all.23.message_ref.mine_ref), channel_id=1, source_target_pairs={{0,1},{1,0},{2,3},{3,2},{4,5},{5,4},{6,7},{7,6},{8,9},{9,8},{10,11... | collective-permute-start | bytes 589832 | tf_op jit(solution)/shard_map/ppermute | solution.py:415

commit v3 on v2

--- a/solution.py
+++ b/solution.py
@@ -246,35 +246,47 @@
             sum(matmul(count_refs[k][...], edge_grad_ref[tiles[k], :]) for k in numbers),
         )
 
+    def start_head(piece):
+        preact = preact_ref[piece, :]
+        grown = jnp.exp(jnp.minimum(preact, 0.0))
+        act = jnp.where(preact > 0.0, preact, grown - 1.0)
+        slope = jnp.where(preact > 0.0, F32(1.0), grown)
+        square = jnp.sum(act * act, axis=1, keepdims=True)
+        along = jnp.sum(act * cot_ref[piece, :].astype(F32), axis=1, keepdims=True)
+        return act, slope, square, along
+
+    def finish_head(piece, act, slope, square, along):
+        scale = lax.rsqrt(square * (1.0 / width) + NORM_EPS)
+        outputs_ref[piece, :] = (act * scale).astype(BF16)
+        pull = along * (scale * scale * scale) * (1.0 / width)
+        grad_pre = (cot_ref[piece, :].astype(F32) * scale - act * pull) * slope
+        low_ref[piece, :] = grad_pre.astype(BF16)
+        return jnp.sum(grad_pre.reshape(PIECE // 8, 8, width), axis=0)
+
+    pieces = [slice(start, start + PIECE) for start in range(0, rows, PIECE)]
     bias_sum = jnp.zeros((8, width), F32)
     copies = []
     before_head(0)
-    for number, nodes in enumerate(tiles):
-        if number + 1 < len(tiles):
-            before_head(number + 1)
-        elif number:
-            w_grad_ref[0], w_grad_ref[1], rest_ref[...] = node_sums(range(number))
-        for start in range(nodes.start, nodes.stop, PIECE):
-            piece = slice(start, start + PIECE)
-            preact = preact_ref[piece, :]
-            cot = cot_ref[piece, :].astype(F32)
-            grown = jnp.exp(jnp.minimum(preact, 0.0))
-            act = jnp.where(preact > 0.0, preact, grown - 1.0)
-            square = jnp.sum(act * act, axis=1, keepdims=True)
-            along = jnp.sum(act * cot, axis=1, keepdims=True)
-            scale = lax.rsqrt(square * (1.0 / width) + NORM_EPS)
-            outputs_ref[piece, :] = (act * scale).astype(BF16)
-            pull = along * (scale * scale * scale) * (1.0 / width)
-            grad_pre = (cot * scale - act * pull) * jnp.where(preact > 0.0, F32(1.0), grown)
-            bias_sum = bias_sum + jnp.sum(grad_pre.reshape(PIECE // 8, 8, width), axis=0)
-            low_ref[piece, :] = grad_pre.astype(BF16)
-        copies += fetch(
-            ((outputs_ref.at[nodes, :], outputs_hbm.at[nodes, :]),), sems.at[pl.ds(number, 1)]
-        )
-        share_column = jnp.broadcast_to(share_ref[:, nodes], (LANES, TILE)).T
-        share_column = jnp.concatenate([share_column] * (width // LANES), axis=1)
-        edge_grad = matmul(low_ref[nodes, :], w_neigh_ref[...], 1, 1) * share_column
-        edge_grad_ref[nodes, :] = edge_grad.astype(BF16)
+    started = start_head(pieces[0])
+    for order, piece in enumerate(pieces):
+        number = piece.start // TILE
+        if piece.start % TILE == 0:
+            if number + 1 < len(tiles):
+                before_head(number + 1)
+            elif number:
+                w_grad_ref[0], w_grad_ref[1], rest_ref[...] = node_sums(range(number))
+        ahead = start_head(pieces[order + 1]) if order + 1 < len(pieces) else None
+        bias_sum = bias_sum + finish_head(piece, *started)
+        started = ahead
+        if piece.stop % TILE == 0:
+            nodes = tiles[number]
+            copies += fetch(
+                ((outputs_ref.at[nodes, :], outputs_hbm.at[nodes, :]),), sems.at[pl.ds(number, 1)]
+            )
+            share_column = jnp.broadcast_to(share_ref[:, nodes], (LANES, TILE)).T
+            share_column = jnp.concatenate([share_column] * (width // LANES), axis=1)
+            edge_grad = matmul(low_ref[nodes, :], w_neigh_ref[...], 1, 1) * share_column
+            edge_grad_ref[nodes, :] = edge_grad.astype(BF16)
 
     w_self_sum, w_neigh_sum, remote = node_sums([len(tiles) - 1])
     if len(tiles) > 1:

time: 49.3 us -> 49.3 us (level)
  no operation moved by 1% of the time
where the time goes in v3:
time: 49.3 us; the launch traced here: 49 us
  blocking collectives  37.3 us (76%)
  Pallas kernels  9.57 us (19%)
  waiting for transfers between devices  0.82 us (2%)
  between operations  0.7 us (1%)
  starting transfers between devices  0.59 us (1%)
    all_to_all x3, blocking collectives, swap(): return lax.all_to_all(array, axes, split_axis=0, concat_axis=0, tiled=True)  37.3 us
    pallas_call x1, Pallas kernels, on_device(): call(functools.partial(joint_kernel, sizes), (pltpu.HBM((rows, width), BF...  2.38 us
    pallas_call x1, Pallas kernels, on_device(): call(functools.partial(own_kernel, tiles), (shape((width, width), BF16),...  2.2 us
    pallas_call x1, Pallas kernels, on_device(): call(functools.partial(pick_kernel, sizes), (shape((doms * tall, width),...  1.75 us
    pallas_call x1, Pallas kernels, on_device(): call(functools.partial(feat_grad_kernel, sizes, slab), shape((rows, width...  1.2 us
  transfers between devices with their start and end apart: 3, of which 2 were waited for; matrix products, arithmetic and copies ran while one was open for 0% of the time, Pallas kernels for 9%

profile of v3, /device:TPU:0, one launch (start us, length us, event | category | flops | bytes accessed | tf_op | source)
XLA Modules:
  0.0 49.0 jit_solution(15989310416553945219)
XLA Ops:
  0.6 1.8 %shard_map.128 = (bf16[64,256]{1,0:T(8,128)(2,1)S(1)}, bf16[16,256]{1,0:T(8,128)(2,1)S(1)}, s32[1,128]{1,0:T(1,128)S(1)}, bf16[1024,256]{1,0:T(8,128)(2,1)S(1)},...) custom-call(s32[2]{0:T(128)} %hub_hbm.1, ...), custom_call_target="tpu_custom_call" | custom-call | flops 67108864 | bytes 524288 | tf_op jit(solution)/shard_map/pallas_call | solution.py:449
  2.4 0.5 %collective-permute-start = (bf16[16,256]{1,0:T(8,128)(2,1)S(1)}, bf16[16,256]{1,0:T(8,128)(2,1)S(1)}, u32[]{:S(2)}, u32[]{:S(2)}) collective-permute-start(bf16[16,256]{1,0:T(8,128)(2,1)S(1)} %get-tuple-element.37), channel_id=1, source_target_pairs={{0,1},{1,0},{2,3},{3,2},{4,5},{5,4},{6,7},{7,6},{8,9},{9,8},{10,11... | collective-permute-start | bytes 24584 | tf_op jit(solution)/shard_map/ppermute | solution.py:427
  2.9 2.2 %shard_map.129 = (bf16[256,256]{1,0:T(8,128)(2,1)S(1)}, bf16[1024,256]{1,0:T(8,128)(2,1)S(1)}, bf16[256,1024]{1,0:T(8,128)(2,1)S(1)}, f32[256,1024]{1,0:T(8,128)...) custom-call(bf16[1024,256]{1,0:T(8,128)(2,1)S(1)} %get-tuple-element, ...), custom_call_target="tpu_custom_call" | custom-call | flops 2415919104 | bytes 5242880 | tf_op jit(solution)/shard_map/pallas_call | solution.py:485
  5.1 0.0 collective-permute-done.hubs_ref
  5.2 15.2 %all_to_all.21 = bf16[16,8,256]{2,1,0:T(8,128)(2,1)S(1)} all-to-all(bf16[16,8,256]{2,1,0:T(8,128)(2,1)S(1)} %bitcast.8), channel_id=1, replica_groups=mesh['dom'=8,'pair'=2,'side'=2] {'dom','pair'}, dimensions={0} | all-to-all | bytes 131072 | tf_op jit(solution)/shard_map/all_to_all | solution.py:423
  20.4 2.4 %shard_map.131 = (bf16[1024,256]{1,0:T(8,128)(2,1)}, f32[256,256]{1,0:T(8,128)S(1)}, f32[128,256]{1,0:T(8,128)S(1)}, bf16[384,256]{1,0:T(8,128)(2,1)S(1)}, bf16[...) custom-call(bf16[128,256]{1,0:T(8,128)(2,1)S(1)} %bitcast.7, ...), custom_call_target="tpu_custom_call" | custom-call | flops 671088640 | bytes 4194304 | tf_op jit(solution)/shard_map/pallas_call | solution.py:512
  22.8 0.1 collective-permute-start.1
  22.9 0.8 %shard_map.132.after_ref.feat_grad_ref = f32[1024,256]{1,0:T(8,128)S(1)} custom-call(bf16[1024,256]{1,0:T(8,128)(2,1)S(1)} %get-tuple-element.56.low_ref, bf16[256,256]{1,0:T(8,128)(2,1)S(1)} %get-tuple-element.39.w_self_ref, bf16[1024,256]{1,0:T(8,128)(2,1)S(1)} %get-tuple-element.57.edge_grad_ref, bf16[1024,256]{1,0:T(8,128)(2,1)S(1)} %get-tuple-element.42.refs_0_, ...), custom_call_target="tpu_custom_call" | custom-call | flops 671088640 | bytes 2097152 | tf_op jit(solution)/shard_map/pallas_call | solution.py:535
  23.7 0.6 %collective-permute-done.1.received_ref = bf16[384,256]{1,0:T(8,128)(2,1)S(1)} collective-permute-done((bf16[384,256]{1,0:T(8,128)(2,1)S(1)}, bf16[384,256]{1,0:T(8,128)(2,1)S(1)}, u32[]{:S(2)}, u32[]{:S(2)}) %collective-permute-start.1) | collective-permute-done | bytes 196640 | tf_op jit(solution)/shard_map/ppermute | solution.py:427
  24.3 10.6 %all_to_all.22.slabs_ref = bf16[16,16,256]{2,1,0:T(8,128)(2,1)S(1)} all-to-all(bf16[16,16,256]{2,1,0:T(8,128)(2,1)S(1)} %shard_map.133), channel_id=1, replica_groups=mesh['dom'=8,'pair'=2,'side'=2] {'dom','pair'}, dimensions={0} | all-to-all | bytes 262144 | tf_op jit(solution)/shard_map/all_to_all | solution.py:423
  34.9 0.2 shard_map.134
  35.1 11.5 %all_to_all.23.message_ref.mine_ref = bf16[16,24,256]{2,1,0:T(8,128)(2,1)S(1)} all-to-all(bf16[16,24,256]{2,1,0:T(8,128)(2,1)S(1)} %shard_map.134), channel_id=1, replica_groups=mesh['dom'=8,'pair'=2,'side'=2] {'dom','pair'}, dimensions={0} | all-to-all | bytes 393216 | tf_op jit(solution)/shard_map/all_to_all | solution.py:423
  46.6 0.0 collective-permute-start.2
  46.6 1.2 %shard_map.135 = bf16[1024,256]{1,0:T(8,128)(2,1)} custom-call(bf16[16,24,256]{2,1,0:T(8,128)(2,1)S(1)} %all_to_all.23.message_ref.mine_ref, s32[1,128]{1,0:T(1,128)S(1)} %get-tuple-element.63.places_ref, f32[1024,256]{1,0:T(8,128)S(1)} %shard_map.132.after_ref.feat_grad_ref), custom_call_target="tpu_custom_call" | custom-call | flops 134217728 | bytes 1572864 | tf_op jit(solution)/shard_map/pallas_call | solution.py:550
  47.8 0.2 collective-permute-done.2.other_ref
  48.0 1.0 %shard_map.136 = (f32[256,256]{1,0:T(8,128)}, f32[256,256]{1,0:T(8,128)}, f32[1,256]{1,0:T(1,128)}) custom-call(bf16[16,24,256]{2,1,0:T(8,128)(2,1)S(1)} %all_to_all.23.message_ref.mine_ref, bf16[16,24,256]{2,1,0:T(8,128)(2,1)S(1)} %collective-permute-done.2.other_ref), custom_call_target="tpu_custom_call" | custom-call | tf_op jit(solution)/shard_map/pallas_call | solution.py:555
  (2 shorter events, 0.1 us)
Async XLA Ops:
  2.4 2.7 %collective-permute-start = (bf16[16,256]{1,0:T(8,128)(2,1)S(1)}, bf16[16,256]{1,0:T(8,128)(2,1)S(1)}, u32[]{:S(2)}, u32[]{:S(2)}) collective-permute-start(bf16[16,256]{1,0:T(8,128)(2,1)S(1)} %get-tuple-element.37), channel_id=1, source_target_pairs={{0,1},{1,0},{2,3},{3,2},{4,5},{5,4},{6,7},{7,6},{8,9},{9,8},{10,11... | collective-permute-start | bytes 24584 | tf_op jit(solution)/shard_map/ppermute | solution.py:427
  22.8 1.5 %collective-permute-start.1 = (bf16[384,256]{1,0:T(8,128)(2,1)S(1)}, bf16[384,256]{1,0:T(8,128)(2,1)S(1)}, u32[]{:S(2)}, u32[]{:S(2)}) collective-permute-start(bf16[384,256]{1,0:T(8,128)(2,1)S(1)} %get-tuple-element.55), channel_id=1, source_target_pairs={{0,1},{1,0},{2,3},{3,2},{4,5},{5,4},{6,7},{7,6},{8,9},{9,8},{10,11... | collective-permute-start | bytes 589832 | tf_op jit(solution)/shard_map/ppermute | solution.py:427
  46.6 1.4 %collective-permute-start.2 = (bf16[16,24,256]{2,1,0:T(8,128)(2,1)S(1)}, bf16[16,24,256]{2,1,0:T(8,128)(2,1)S(1)}, u32[]{:S(2)}, u32[]{:S(2)}) collective-permute-start(bf16[16,24,256]{2,1,0:T(8,128)(2,1)S(1)} %all_to_all.23.message_ref.mine_ref), channel_id=1, source_target_pairs={{0,1},{1,0},{2,3},{3,2},{4,5},{5,4},{6,7},{7,6},{8,9},{9,8},{10,11... | collective-permute-start | bytes 589832 | tf_op jit(solution)/shard_map/ppermute | solution.py:427

commit v4 on v2

--- a/solution.py
+++ b/solution.py
@@ -139,10 +139,11 @@
         hot = [jnp.where(numbers == low[k], BF16(1.0), BF16(0.0)) for k in range(fanout)]
 
         def count(block):
-            total = hot[0] * hot_ref[block * fanout]
-            for k in range(1, fanout):
-                total = total + hot[k] * hot_ref[block * fanout + k]
-            return total
+            terms = [hot[k] * hot_ref[block * fanout + k] for k in range(fanout)]
+            while len(terms) > 1:
+                pairs = [left + right for left, right in zip(terms[::2], terms[1::2])]
+                terms = pairs + terms[2 * len(pairs) :]
+            return terms[0]
 
         for block in range(rows // LANES):
             first = block * LANES + strip
@@ -259,13 +260,13 @@
             preact = preact_ref[piece, :]
             cot = cot_ref[piece, :].astype(F32)
             grown = jnp.exp(jnp.minimum(preact, 0.0))
-            act = jnp.where(preact > 0.0, preact, grown - 1.0)
+            act = jnp.maximum(preact, 0.0) + (grown - 1.0)
             square = jnp.sum(act * act, axis=1, keepdims=True)
             along = jnp.sum(act * cot, axis=1, keepdims=True)
             scale = lax.rsqrt(square * (1.0 / width) + NORM_EPS)
             outputs_ref[piece, :] = (act * scale).astype(BF16)
             pull = along * (scale * scale * scale) * (1.0 / width)
-            grad_pre = (cot * scale - act * pull) * jnp.where(preact > 0.0, F32(1.0), grown)
+            grad_pre = (cot * scale - act * pull) * grown
             bias_sum = bias_sum + jnp.sum(grad_pre.reshape(PIECE // 8, 8, width), axis=0)
             low_ref[piece, :] = grad_pre.astype(BF16)
         copies += fetch(

time: 49.3 us -> 50 us (1.014)
  Pallas kernels: 9.56 us -> 10.3 us
    pallas_call x1, Pallas kernels: 2.2 us -> 2.94 us  [on_device(): call(functools.partial(own_kernel, tiles), (shape((width, width), BF16),...]
  transfers between devices with their start and end apart: 3 -> 3, of which waited for: 2 -> 2; matrix products, arithmetic and copies ran while one was open for 0% -> 0% of each run, Pallas kernels for 9% -> 10%
where the time goes in v4:
time: 50 us; the launch traced here: 49.7 us
  blocking collectives  37.3 us (75%)
  Pallas kernels  10.3 us (21%)
  waiting for transfers between devices  0.81 us (2%)
  between operations  0.7 us (1%)
  starting transfers between devices  0.59 us (1%)
    all_to_all x3, blocking collectives, swap(): return lax.all_to_all(array, axes, split_axis=0, concat_axis=0, tiled=True)  37.3 us
    pallas_call x1, Pallas kernels, on_device(): call(functools.partial(own_kernel, tiles), (shape((width, width), BF16),...  2.94 us
    pallas_call x1, Pallas kernels, on_device(): call(functools.partial(joint_kernel, sizes), (pltpu.HBM((rows, width), BF...  2.36 us
    pallas_call x1, Pallas kernels, on_device(): call(functools.partial(pick_kernel, sizes), (shape((doms * tall, width),...  1.76 us
    pallas_call x1, Pallas kernels, on_device(): call(functools.partial(feat_grad_kernel, sizes, slab), shape((rows, width...  1.21 us
  transfers between devices with their start and end apart: 3, of which 2 were waited for; matrix products, arithmetic and copies ran while one was open for 0% of the time, Pallas kernels for 10%

profile of v4, /device:TPU:0, one launch (start us, length us, event | category | flops | bytes accessed | tf_op | source)
XLA Modules:
  0.0 49.7 jit_solution(8481829713943945904)
XLA Ops:
  0.6 1.8 %shard_map.128 = (bf16[64,256]{1,0:T(8,128)(2,1)S(1)}, bf16[16,256]{1,0:T(8,128)(2,1)S(1)}, s32[1,128]{1,0:T(1,128)S(1)}, bf16[1024,256]{1,0:T(8,128)(2,1)S(1)},...) custom-call(s32[2]{0:T(128)} %hub_hbm.1, ...), custom_call_target="tpu_custom_call" | custom-call | flops 67108864 | bytes 524288 | tf_op jit(solution)/shard_map/pallas_call | solution.py:438
  2.4 0.5 %collective-permute-start = (bf16[16,256]{1,0:T(8,128)(2,1)S(1)}, bf16[16,256]{1,0:T(8,128)(2,1)S(1)}, u32[]{:S(2)}, u32[]{:S(2)}) collective-permute-start(bf16[16,256]{1,0:T(8,128)(2,1)S(1)} %get-tuple-element.37), channel_id=1, source_target_pairs={{0,1},{1,0},{2,3},{3,2},{4,5},{5,4},{6,7},{7,6},{8,9},{9,8},{10,11... | collective-permute-start | bytes 24584 | tf_op jit(solution)/shard_map/ppermute | solution.py:416
  2.9 2.9 %shard_map.129 = (bf16[256,256]{1,0:T(8,128)(2,1)S(1)}, bf16[1024,256]{1,0:T(8,128)(2,1)S(1)}, bf16[256,1024]{1,0:T(8,128)(2,1)S(1)}, f32[256,1024]{1,0:T(8,128)...) custom-call(bf16[1024,256]{1,0:T(8,128)(2,1)S(1)} %get-tuple-element, ...), custom_call_target="tpu_custom_call" | custom-call | flops 2415919104 | bytes 5242880 | tf_op jit(solution)/shard_map/pallas_call | solution.py:474
  5.9 0.0 collective-permute-done.hubs_ref
  5.9 15.2 %all_to_all.21 = bf16[16,8,256]{2,1,0:T(8,128)(2,1)S(1)} all-to-all(bf16[16,8,256]{2,1,0:T(8,128)(2,1)S(1)} %bitcast.8), channel_id=1, replica_groups=mesh['dom'=8,'pair'=2,'side'=2] {'dom','pair'}, dimensions={0} | all-to-all | bytes 131072 | tf_op jit(solution)/shard_map/all_to_all | solution.py:412
  21.1 2.4 %shard_map.131 = (bf16[1024,256]{1,0:T(8,128)(2,1)}, f32[256,256]{1,0:T(8,128)S(1)}, f32[128,256]{1,0:T(8,128)S(1)}, bf16[384,256]{1,0:T(8,128)(2,1)S(1)}, bf16[...) custom-call(bf16[128,256]{1,0:T(8,128)(2,1)S(1)} %bitcast.7, ...), custom_call_target="tpu_custom_call" | custom-call | flops 671088640 | bytes 4194304 | tf_op jit(solution)/shard_map/pallas_call | solution.py:501
  23.5 0.1 collective-permute-start.1
  23.6 0.8 %shard_map.132.after_ref.feat_grad_ref = f32[1024,256]{1,0:T(8,128)S(1)} custom-call(bf16[1024,256]{1,0:T(8,128)(2,1)S(1)} %get-tuple-element.56.low_ref, bf16[256,256]{1,0:T(8,128)(2,1)S(1)} %get-tuple-element.39.w_self_ref, bf16[1024,256]{1,0:T(8,128)(2,1)S(1)} %get-tuple-element.57.edge_grad_ref, bf16[1024,256]{1,0:T(8,128)(2,1)S(1)} %get-tuple-element.42.refs_0_, ...), custom_call_target="tpu_custom_call" | custom-call | flops 671088640 | bytes 2097152 | tf_op jit(solution)/shard_map/pallas_call | solution.py:524
  24.4 0.6 %collective-permute-done.1.received_ref = bf16[384,256]{1,0:T(8,128)(2,1)S(1)} collective-permute-done((bf16[384,256]{1,0:T(8,128)(2,1)S(1)}, bf16[384,256]{1,0:T(8,128)(2,1)S(1)}, u32[]{:S(2)}, u32[]{:S(2)}) %collective-permute-start.1) | collective-permute-done | bytes 196640 | tf_op jit(solution)/shard_map/ppermute | solution.py:416
  25.0 10.6 %all_to_all.22.slabs_ref = bf16[16,16,256]{2,1,0:T(8,128)(2,1)S(1)} all-to-all(bf16[16,16,256]{2,1,0:T(8,128)(2,1)S(1)} %shard_map.133), channel_id=1, replica_groups=mesh['dom'=8,'pair'=2,'side'=2] {'dom','pair'}, dimensions={0} | all-to-all | bytes 262144 | tf_op jit(solution)/shard_map/all_to_all | solution.py:412
  35.6 0.2 shard_map.134
  35.8 11.5 %all_to_all.23.message_ref.mine_ref = bf16[16,24,256]{2,1,0:T(8,128)(2,1)S(1)} all-to-all(bf16[16,24,256]{2,1,0:T(8,128)(2,1)S(1)} %shard_map.134), channel_id=1, replica_groups=mesh['dom'=8,'pair'=2,'side'=2] {'dom','pair'}, dimensions={0} | all-to-all | bytes 393216 | tf_op jit(solution)/shard_map/all_to_all | solution.py:412
  47.3 0.0 collective-permute-start.2
  47.3 1.2 %shard_map.135 = bf16[1024,256]{1,0:T(8,128)(2,1)} custom-call(bf16[16,24,256]{2,1,0:T(8,128)(2,1)S(1)} %all_to_all.23.message_ref.mine_ref, s32[1,128]{1,0:T(1,128)S(1)} %get-tuple-element.63.places_ref, f32[1024,256]{1,0:T(8,128)S(1)} %shard_map.132.after_ref.feat_grad_ref), custom_call_target="tpu_custom_call" | custom-call | flops 134217728 | bytes 1572864 | tf_op jit(solution)/shard_map/pallas_call | solution.py:539
  48.5 0.2 collective-permute-done.2.other_ref
  48.7 1.0 %shard_map.136 = (f32[256,256]{1,0:T(8,128)}, f32[256,256]{1,0:T(8,128)}, f32[1,256]{1,0:T(1,128)}) custom-call(bf16[16,24,256]{2,1,0:T(8,128)(2,1)S(1)} %all_to_all.23.message_ref.mine_ref, bf16[16,24,256]{2,1,0:T(8,128)(2,1)S(1)} %collective-permute-done.2.other_ref), custom_call_target="tpu_custom_call" | custom-call | tf_op jit(solution)/shard_map/pallas_call | solution.py:544
  (2 shorter events, 0.1 us)
Async XLA Ops:
  2.4 3.5 %collective-permute-start = (bf16[16,256]{1,0:T(8,128)(2,1)S(1)}, bf16[16,256]{1,0:T(8,128)(2,1)S(1)}, u32[]{:S(2)}, u32[]{:S(2)}) collective-permute-start(bf16[16,256]{1,0:T(8,128)(2,1)S(1)} %get-tuple-element.37), channel_id=1, source_target_pairs={{0,1},{1,0},{2,3},{3,2},{4,5},{5,4},{6,7},{7,6},{8,9},{9,8},{10,11... | collective-permute-start | bytes 24584 | tf_op jit(solution)/shard_map/ppermute | solution.py:416
  23.5 1.5 %collective-permute-start.1 = (bf16[384,256]{1,0:T(8,128)(2,1)S(1)}, bf16[384,256]{1,0:T(8,128)(2,1)S(1)}, u32[]{:S(2)}, u32[]{:S(2)}) collective-permute-start(bf16[384,256]{1,0:T(8,128)(2,1)S(1)} %get-tuple-element.55), channel_id=1, source_target_pairs={{0,1},{1,0},{2,3},{3,2},{4,5},{5,4},{6,7},{7,6},{8,9},{9,8},{10,11... | collective-permute-start | bytes 589832 | tf_op jit(solution)/shard_map/ppermute | solution.py:416
  47.3 1.4 %collective-permute-start.2 = (bf16[16,24,256]{2,1,0:T(8,128)(2,1)S(1)}, bf16[16,24,256]{2,1,0:T(8,128)(2,1)S(1)}, u32[]{:S(2)}, u32[]{:S(2)}) collective-permute-start(bf16[16,24,256]{2,1,0:T(8,128)(2,1)S(1)} %all_to_all.23.message_ref.mine_ref), channel_id=1, source_target_pairs={{0,1},{1,0},{2,3},{3,2},{4,5},{5,4},{6,7},{7,6},{8,9},{9,8},{10,11... | collective-permute-start | bytes 589832 | tf_op jit(solution)/shard_map/ppermute | solution.py:416

commit v5 on v2

--- a/solution.py
+++ b/solution.py
@@ -134,30 +134,34 @@
     for block in range(highs):
         for k in range(fanout):
             hot_ref[block * fanout + k] = jnp.where(high[k] == block, BF16(1.0), BF16(0.0))
-    for strip in range(0, LANES, STRIP):
-        numbers = (iota((STRIP, TILE), 0) + strip).astype(jnp.int16)
-        hot = [jnp.where(numbers == low[k], BF16(1.0), BF16(0.0)) for k in range(fanout)]
+    for strip in range(0, LANES, 2 * STRIP):
+        hot = []
+        for start in (strip, strip + STRIP):
+            numbers = (iota((STRIP, TILE), 0) + start).astype(jnp.int16)
+            hot.append([jnp.where(numbers == low[k], BF16(1.0), BF16(0.0)) for k in range(fanout)])
 
         def count(block):
-            total = hot[0] * hot_ref[block * fanout]
+            part = hot_ref[block * fanout]
+            totals = [hot[0][0] * part, hot[1][0] * part]
             for k in range(1, fanout):
-                total = total + hot[k] * hot_ref[block * fanout + k]
-            return total
+                part = hot_ref[block * fanout + k]
+                totals = [total + each[k] * part for total, each in zip(totals, hot)]
+            return jnp.concatenate(totals, axis=0)
 
         for block in range(rows // LANES):
             first = block * LANES + strip
-            own_count_ref[first : first + STRIP, :] = count(block)
+            own_count_ref[first : first + 2 * STRIP, :] = count(block)
         far = far_count_ref.shape[0] // LANES
         if far <= 4:
             for block in range(far):
                 first = block * LANES + strip
-                far_count_ref[first : first + STRIP, :] = count(rows // LANES + block)
+                far_count_ref[first : first + 2 * STRIP, :] = count(rows // LANES + block)
         else:
 
             @pl.loop(0, far)
             def far_block(block):
-                first = pl.multiple_of(block * LANES + strip, STRIP)
-                far_count_ref[pl.ds(first, STRIP), :] = count(rows // LANES + block)
+                first = pl.multiple_of(block * LANES + strip, 2 * STRIP)
+                far_count_ref[pl.ds(first, 2 * STRIP), :] = count(rows // LANES + block)
 
 
 def find_slots(sizes, degree_ref, edge_ref, slot_ref, share_ref):

time: 49.3 us -> 49.3 us (level)
  no operation moved by 1% of the time
where the time goes in v5:
time: 49.3 us; the launch traced here: 49 us
  blocking collectives  37.3 us (76%)
  Pallas kernels  9.56 us (19%)
  waiting for transfers between devices  0.81 us (2%)
  between operations  0.7 us (1%)
  starting transfers between devices  0.59 us (1%)
    all_to_all x3, blocking collectives, swap(): return lax.all_to_all(array, axes, split_axis=0, concat_axis=0, tiled=True)  37.3 us
    pallas_call x1, Pallas kernels, on_device(): call(functools.partial(joint_kernel, sizes), (pltpu.HBM((rows, width), BF...  2.37 us
    pallas_call x1, Pallas kernels, on_device(): call(functools.partial(own_kernel, tiles), (shape((width, width), BF16),...  2.2 us
    pallas_call x1, Pallas kernels, on_device(): call(functools.partial(pick_kernel, sizes), (shape((doms * tall, width),...  1.75 us
    pallas_call x1, Pallas kernels, on_device(): call(functools.partial(feat_grad_kernel, sizes, slab), shape((rows, width...  1.2 us
  transfers between devices with their start and end apart: 3, of which 2 were waited for; matrix products, arithmetic and copies ran while one was open for 0% of the time, Pallas kernels for 9%

profile of v5, /device:TPU:0, one launch (start us, length us, event | category | flops | bytes accessed | tf_op | source)
XLA Modules:
  0.0 49.0 jit_solution(11374798619622910660)
XLA Ops:
  0.6 1.8 %shard_map.128 = (bf16[64,256]{1,0:T(8,128)(2,1)S(1)}, bf16[16,256]{1,0:T(8,128)(2,1)S(1)}, s32[1,128]{1,0:T(1,128)S(1)}, bf16[1024,256]{1,0:T(8,128)(2,1)S(1)},...) custom-call(s32[2]{0:T(128)} %hub_hbm.1, ...), custom_call_target="tpu_custom_call" | custom-call | flops 67108864 | bytes 524288 | tf_op jit(solution)/shard_map/pallas_call | solution.py:441
  2.4 0.5 %collective-permute-start = (bf16[16,256]{1,0:T(8,128)(2,1)S(1)}, bf16[16,256]{1,0:T(8,128)(2,1)S(1)}, u32[]{:S(2)}, u32[]{:S(2)}) collective-permute-start(bf16[16,256]{1,0:T(8,128)(2,1)S(1)} %get-tuple-element.37), channel_id=1, source_target_pairs={{0,1},{1,0},{2,3},{3,2},{4,5},{5,4},{6,7},{7,6},{8,9},{9,8},{10,11... | collective-permute-start | bytes 24584 | tf_op jit(solution)/shard_map/ppermute | solution.py:419
  2.9 2.2 %shard_map.129 = (bf16[256,256]{1,0:T(8,128)(2,1)S(1)}, bf16[1024,256]{1,0:T(8,128)(2,1)S(1)}, bf16[256,1024]{1,0:T(8,128)(2,1)S(1)}, f32[256,1024]{1,0:T(8,128)...) custom-call(bf16[1024,256]{1,0:T(8,128)(2,1)S(1)} %get-tuple-element, ...), custom_call_target="tpu_custom_call" | custom-call | flops 2415919104 | bytes 5242880 | tf_op jit(solution)/shard_map/pallas_call | solution.py:477
  5.1 0.0 collective-permute-done.hubs_ref
  5.2 15.2 %all_to_all.21 = bf16[16,8,256]{2,1,0:T(8,128)(2,1)S(1)} all-to-all(bf16[16,8,256]{2,1,0:T(8,128)(2,1)S(1)} %bitcast.8), channel_id=1, replica_groups=mesh['dom'=8,'pair'=2,'side'=2] {'dom','pair'}, dimensions={0} | all-to-all | bytes 131072 | tf_op jit(solution)/shard_map/all_to_all | solution.py:415
  20.4 2.4 %shard_map.131 = (bf16[1024,256]{1,0:T(8,128)(2,1)}, f32[256,256]{1,0:T(8,128)S(1)}, f32[128,256]{1,0:T(8,128)S(1)}, bf16[384,256]{1,0:T(8,128)(2,1)S(1)}, bf16[...) custom-call(bf16[128,256]{1,0:T(8,128)(2,1)S(1)} %bitcast.7, ...), custom_call_target="tpu_custom_call" | custom-call | flops 671088640 | bytes 4194304 | tf_op jit(solution)/shard_map/pallas_call | solution.py:504
  22.8 0.1 collective-permute-start.1
  22.8 0.8 %shard_map.132.after_ref.feat_grad_ref = f32[1024,256]{1,0:T(8,128)S(1)} custom-call(bf16[1024,256]{1,0:T(8,128)(2,1)S(1)} %get-tuple-element.56.low_ref, bf16[256,256]{1,0:T(8,128)(2,1)S(1)} %get-tuple-element.39.w_self_ref, bf16[1024,256]{1,0:T(8,128)(2,1)S(1)} %get-tuple-element.57.edge_grad_ref, bf16[1024,256]{1,0:T(8,128)(2,1)S(1)} %get-tuple-element.42.refs_0_, ...), custom_call_target="tpu_custom_call" | custom-call | flops 671088640 | bytes 2097152 | tf_op jit(solution)/shard_map/pallas_call | solution.py:527
  23.7 0.6 %collective-permute-done.1.received_ref = bf16[384,256]{1,0:T(8,128)(2,1)S(1)} collective-permute-done((bf16[384,256]{1,0:T(8,128)(2,1)S(1)}, bf16[384,256]{1,0:T(8,128)(2,1)S(1)}, u32[]{:S(2)}, u32[]{:S(2)}) %collective-permute-start.1) | collective-permute-done | bytes 196640 | tf_op jit(solution)/shard_map/ppermute | solution.py:419
  24.3 10.6 %all_to_all.22.slabs_ref = bf16[16,16,256]{2,1,0:T(8,128)(2,1)S(1)} all-to-all(bf16[16,16,256]{2,1,0:T(8,128)(2,1)S(1)} %shard_map.133), channel_id=1, replica_groups=mesh['dom'=8,'pair'=2,'side'=2] {'dom','pair'}, dimensions={0} | all-to-all | bytes 262144 | tf_op jit(solution)/shard_map/all_to_all | solution.py:415
  34.9 0.2 shard_map.134
  35.1 11.5 %all_to_all.23.message_ref.mine_ref = bf16[16,24,256]{2,1,0:T(8,128)(2,1)S(1)} all-to-all(bf16[16,24,256]{2,1,0:T(8,128)(2,1)S(1)} %shard_map.134), channel_id=1, replica_groups=mesh['dom'=8,'pair'=2,'side'=2] {'dom','pair'}, dimensions={0} | all-to-all | bytes 393216 | tf_op jit(solution)/shard_map/all_to_all | solution.py:415
  46.6 0.0 collective-permute-start.2
  46.6 1.2 %shard_map.135 = bf16[1024,256]{1,0:T(8,128)(2,1)} custom-call(bf16[16,24,256]{2,1,0:T(8,128)(2,1)S(1)} %all_to_all.23.message_ref.mine_ref, s32[1,128]{1,0:T(1,128)S(1)} %get-tuple-element.63.places_ref, f32[1024,256]{1,0:T(8,128)S(1)} %shard_map.132.after_ref.feat_grad_ref), custom_call_target="tpu_custom_call" | custom-call | flops 134217728 | bytes 1572864 | tf_op jit(solution)/shard_map/pallas_call | solution.py:542
  47.8 0.2 collective-permute-done.2.other_ref
  48.0 1.0 %shard_map.136 = (f32[256,256]{1,0:T(8,128)}, f32[256,256]{1,0:T(8,128)}, f32[1,256]{1,0:T(1,128)}) custom-call(bf16[16,24,256]{2,1,0:T(8,128)(2,1)S(1)} %all_to_all.23.message_ref.mine_ref, bf16[16,24,256]{2,1,0:T(8,128)(2,1)S(1)} %collective-permute-done.2.other_ref), custom_call_target="tpu_custom_call" | custom-call | tf_op jit(solution)/shard_map/pallas_call | solution.py:547
  (2 shorter events, 0.1 us)
Async XLA Ops:
  2.4 2.7 %collective-permute-start = (bf16[16,256]{1,0:T(8,128)(2,1)S(1)}, bf16[16,256]{1,0:T(8,128)(2,1)S(1)}, u32[]{:S(2)}, u32[]{:S(2)}) collective-permute-start(bf16[16,256]{1,0:T(8,128)(2,1)S(1)} %get-tuple-element.37), channel_id=1, source_target_pairs={{0,1},{1,0},{2,3},{3,2},{4,5},{5,4},{6,7},{7,6},{8,9},{9,8},{10,11... | collective-permute-start | bytes 24584 | tf_op jit(solution)/shard_map/ppermute | solution.py:419
  22.8 1.5 %collective-permute-start.1 = (bf16[384,256]{1,0:T(8,128)(2,1)S(1)}, bf16[384,256]{1,0:T(8,128)(2,1)S(1)}, u32[]{:S(2)}, u32[]{:S(2)}) collective-permute-start(bf16[384,256]{1,0:T(8,128)(2,1)S(1)} %get-tuple-element.55), channel_id=1, source_target_pairs={{0,1},{1,0},{2,3},{3,2},{4,5},{5,4},{6,7},{7,6},{8,9},{9,8},{10,11... | collective-permute-start | bytes 589832 | tf_op jit(solution)/shard_map/ppermute | solution.py:419
  46.6 1.4 %collective-permute-start.2 = (bf16[16,24,256]{2,1,0:T(8,128)(2,1)S(1)}, bf16[16,24,256]{2,1,0:T(8,128)(2,1)S(1)}, u32[]{:S(2)}, u32[]{:S(2)}) collective-permute-start(bf16[16,24,256]{2,1,0:T(8,128)(2,1)S(1)} %all_to_all.23.message_ref.mine_ref), channel_id=1, source_target_pairs={{0,1},{1,0},{2,3},{3,2},{4,5},{5,4},{6,7},{7,6},{8,9},{9,8},{10,11... | collective-permute-start | bytes 589832 | tf_op jit(solution)/shard_map/ppermute | solution.py:419

commit v6 on v5

--- a/solution.py
+++ b/solution.py
@@ -244,10 +244,11 @@
     def node_sums(numbers):
         nodes = slice(tiles[numbers[0]].start, tiles[numbers[-1]].stop)
         low = low_ref[nodes, :]
+        counts = jnp.concatenate([count_refs[k][...] for k in numbers], axis=1)
         return (
             matmul(turned_ref[:, nodes], low),
             matmul(mean_ref[:, nodes], low),
-            sum(matmul(count_refs[k][...], edge_grad_ref[tiles[k], :]) for k in numbers),
+            matmul(counts, edge_grad_ref[nodes, :]),
         )
 
     bias_sum = jnp.zeros((8, width), F32)
@@ -308,11 +309,10 @@
     *count_refs, feat_grad_ref = refs
     for first in range(0, low_ref.shape[0], TILE):
         nodes = slice(first, first + TILE)
-        total = matmul(low_ref[nodes, :], w_self_ref[...], 1, 1)
-        for number, count_ref in enumerate(count_refs):
-            edges = edge_grad_ref[number * TILE : (number + 1) * TILE, :]
-            total = total + matmul(count_ref[nodes, :], edges)
-        feat_grad_ref[nodes, :] = total
+        counts = jnp.concatenate([count_ref[nodes, :] for count_ref in count_refs], axis=1)
+        feat_grad_ref[nodes, :] = matmul(counts, edge_grad_ref[...]) + matmul(
+            low_ref[nodes, :], w_self_ref[...], 1, 1
+        )
 
 
 def side_sum_kernel(own_ref, received_ref, after_ref, message_ref):

time: 49.3 us -> 49.3 us (level)
  no operation moved by 1% of the time
where the time goes in v6:
time: 49.3 us; the launch traced here: 49 us
  blocking collectives  37.3 us (76%)
  Pallas kernels  9.6 us (19%)
  waiting for transfers between devices  0.78 us (2%)
  between operations  0.7 us (1%)
  starting transfers between devices  0.59 us (1%)
    all_to_all x3, blocking collectives, swap(): return lax.all_to_all(array, axes, split_axis=0, concat_axis=0, tiled=True)  37.3 us
    pallas_call x1, Pallas kernels, on_device(): call(functools.partial(joint_kernel, sizes), (pltpu.HBM((rows, width), BF...  2.37 us
    pallas_call x1, Pallas kernels, on_device(): call(functools.partial(own_kernel, tiles), (shape((width, width), BF16),...  2.2 us
    pallas_call x1, Pallas kernels, on_device(): call(functools.partial(pick_kernel, sizes), (shape((doms * tall, width),...  1.75 us
    pallas_call x1, Pallas kernels, on_device(): call(functools.partial(feat_grad_kernel, sizes, slab), shape((rows, width...  1.2 us
  transfers between devices with their start and end apart: 3, of which 2 were waited for; matrix products, arithmetic and copies ran while one was open for 0% of the time, Pallas kernels for 9%

profile of v6, /device:TPU:0, one launch (start us, length us, event | category | flops | bytes accessed | tf_op | source)
XLA Modules:
  0.0 49.0 jit_solution(1366649488372957301)
XLA Ops:
  0.6 1.8 %shard_map.128 = (bf16[64,256]{1,0:T(8,128)(2,1)S(1)}, bf16[16,256]{1,0:T(8,128)(2,1)S(1)}, s32[1,128]{1,0:T(1,128)S(1)}, bf16[1024,256]{1,0:T(8,128)(2,1)S(1)},...) custom-call(s32[2]{0:T(128)} %hub_hbm.1, ...), custom_call_target="tpu_custom_call" | custom-call | flops 67108864 | bytes 524288 | tf_op jit(solution)/shard_map/pallas_call | solution.py:441
  2.4 0.5 %collective-permute-start = (bf16[16,256]{1,0:T(8,128)(2,1)S(1)}, bf16[16,256]{1,0:T(8,128)(2,1)S(1)}, u32[]{:S(2)}, u32[]{:S(2)}) collective-permute-start(bf16[16,256]{1,0:T(8,128)(2,1)S(1)} %get-tuple-element.37), channel_id=1, source_target_pairs={{0,1},{1,0},{2,3},{3,2},{4,5},{5,4},{6,7},{7,6},{8,9},{9,8},{10,11... | collective-permute-start | bytes 24584 | tf_op jit(solution)/shard_map/ppermute | solution.py:419
  2.9 2.2 %shard_map.129 = (bf16[256,256]{1,0:T(8,128)(2,1)S(1)}, bf16[1024,256]{1,0:T(8,128)(2,1)S(1)}, bf16[256,1024]{1,0:T(8,128)(2,1)S(1)}, f32[256,1024]{1,0:T(8,128)...) custom-call(bf16[1024,256]{1,0:T(8,128)(2,1)S(1)} %get-tuple-element, ...), custom_call_target="tpu_custom_call" | custom-call | flops 2415919104 | bytes 5242880 | tf_op jit(solution)/shard_map/pallas_call | solution.py:477
  5.1 0.0 collective-permute-done.hubs_ref
  5.2 15.2 %all_to_all.21 = bf16[16,8,256]{2,1,0:T(8,128)(2,1)S(1)} all-to-all(bf16[16,8,256]{2,1,0:T(8,128)(2,1)S(1)} %bitcast.8), channel_id=1, replica_groups=mesh['dom'=8,'pair'=2,'side'=2] {'dom','pair'}, dimensions={0} | all-to-all | bytes 131072 | tf_op jit(solution)/shard_map/all_to_all | solution.py:415
  20.4 2.4 %shard_map.131 = (bf16[1024,256]{1,0:T(8,128)(2,1)}, f32[256,256]{1,0:T(8,128)S(1)}, f32[128,256]{1,0:T(8,128)S(1)}, bf16[384,256]{1,0:T(8,128)(2,1)S(1)}, bf16[...) custom-call(bf16[128,256]{1,0:T(8,128)(2,1)S(1)} %bitcast.7, ...), custom_call_target="tpu_custom_call" | custom-call | flops 671088640 | bytes 4194304 | tf_op jit(solution)/shard_map/pallas_call | solution.py:504
  22.8 0.1 collective-permute-start.1
  22.8 0.9 %shard_map.132.after_ref.feat_grad_ref = f32[1024,256]{1,0:T(8,128)S(1)} custom-call(bf16[1024,256]{1,0:T(8,128)(2,1)S(1)} %get-tuple-element.56.low_ref, bf16[256,256]{1,0:T(8,128)(2,1)S(1)} %get-tuple-element.39.w_self_ref, bf16[1024,256]{1,0:T(8,128)(2,1)S(1)} %get-tuple-element.57.edge_grad_ref, bf16[1024,256]{1,0:T(8,128)(2,1)S(1)} %get-tuple-element.42.refs_0_, ...), custom_call_target="tpu_custom_call" | custom-call | flops 671088640 | bytes 2097152 | tf_op jit(solution)/shard_map/pallas_call | solution.py:527
  23.7 0.5 %collective-permute-done.1.received_ref = bf16[384,256]{1,0:T(8,128)(2,1)S(1)} collective-permute-done((bf16[384,256]{1,0:T(8,128)(2,1)S(1)}, bf16[384,256]{1,0:T(8,128)(2,1)S(1)}, u32[]{:S(2)}, u32[]{:S(2)}) %collective-permute-start.1) | collective-permute-done | bytes 196640 | tf_op jit(solution)/shard_map/ppermute | solution.py:419
  24.3 10.6 %all_to_all.22.slabs_ref = bf16[16,16,256]{2,1,0:T(8,128)(2,1)S(1)} all-to-all(bf16[16,16,256]{2,1,0:T(8,128)(2,1)S(1)} %shard_map.133), channel_id=1, replica_groups=mesh['dom'=8,'pair'=2,'side'=2] {'dom','pair'}, dimensions={0} | all-to-all | bytes 262144 | tf_op jit(solution)/shard_map/all_to_all | solution.py:415
  34.9 0.2 shard_map.134
  35.1 11.5 %all_to_all.23.message_ref.mine_ref = bf16[16,24,256]{2,1,0:T(8,128)(2,1)S(1)} all-to-all(bf16[16,24,256]{2,1,0:T(8,128)(2,1)S(1)} %shard_map.134), channel_id=1, replica_groups=mesh['dom'=8,'pair'=2,'side'=2] {'dom','pair'}, dimensions={0} | all-to-all | bytes 393216 | tf_op jit(solution)/shard_map/all_to_all | solution.py:415
  46.6 0.0 collective-permute-start.2
  46.6 1.2 %shard_map.135 = bf16[1024,256]{1,0:T(8,128)(2,1)} custom-call(bf16[16,24,256]{2,1,0:T(8,128)(2,1)S(1)} %all_to_all.23.message_ref.mine_ref, s32[1,128]{1,0:T(1,128)S(1)} %get-tuple-element.63.places_ref, f32[1024,256]{1,0:T(8,128)S(1)} %shard_map.132.after_ref.feat_grad_ref), custom_call_target="tpu_custom_call" | custom-call | flops 134217728 | bytes 1572864 | tf_op jit(solution)/shard_map/pallas_call | solution.py:542
  47.8 0.2 collective-permute-done.2.other_ref
  48.0 1.0 %shard_map.136 = (f32[256,256]{1,0:T(8,128)}, f32[256,256]{1,0:T(8,128)}, f32[1,256]{1,0:T(1,128)}) custom-call(bf16[16,24,256]{2,1,0:T(8,128)(2,1)S(1)} %all_to_all.23.message_ref.mine_ref, bf16[16,24,256]{2,1,0:T(8,128)(2,1)S(1)} %collective-permute-done.2.other_ref), custom_call_target="tpu_custom_call" | custom-call | tf_op jit(solution)/shard_map/pallas_call | solution.py:547
  (2 shorter events, 0.1 us)
Async XLA Ops:
  2.4 2.7 %collective-permute-start = (bf16[16,256]{1,0:T(8,128)(2,1)S(1)}, bf16[16,256]{1,0:T(8,128)(2,1)S(1)}, u32[]{:S(2)}, u32[]{:S(2)}) collective-permute-start(bf16[16,256]{1,0:T(8,128)(2,1)S(1)} %get-tuple-element.37), channel_id=1, source_target_pairs={{0,1},{1,0},{2,3},{3,2},{4,5},{5,4},{6,7},{7,6},{8,9},{9,8},{10,11... | collective-permute-start | bytes 24584 | tf_op jit(solution)/shard_map/ppermute | solution.py:419
  22.8 1.5 %collective-permute-start.1 = (bf16[384,256]{1,0:T(8,128)(2,1)S(1)}, bf16[384,256]{1,0:T(8,128)(2,1)S(1)}, u32[]{:S(2)}, u32[]{:S(2)}) collective-permute-start(bf16[384,256]{1,0:T(8,128)(2,1)S(1)} %get-tuple-element.55), channel_id=1, source_target_pairs={{0,1},{1,0},{2,3},{3,2},{4,5},{5,4},{6,7},{7,6},{8,9},{9,8},{10,11... | collective-permute-start | bytes 589832 | tf_op jit(solution)/shard_map/ppermute | solution.py:419
  46.6 1.4 %collective-permute-start.2 = (bf16[16,24,256]{2,1,0:T(8,128)(2,1)S(1)}, bf16[16,24,256]{2,1,0:T(8,128)(2,1)S(1)}, u32[]{:S(2)}, u32[]{:S(2)}) collective-permute-start(bf16[16,24,256]{2,1,0:T(8,128)(2,1)S(1)} %all_to_all.23.message_ref.mine_ref), channel_id=1, source_target_pairs={{0,1},{1,0},{2,3},{3,2},{4,5},{5,4},{6,7},{7,6},{8,9},{9,8},{10,11... | collective-permute-start | bytes 589832 | tf_op jit(solution)/shard_map/ppermute | solution.py:419

commit v7 on v5

--- a/solution.py
+++ b/solution.py
@@ -292,11 +292,14 @@
     bias_sum = jnp.broadcast_to(jnp.sum(bias_sum, axis=0, keepdims=True), (tall, width))
     bias_high = bias_sum.astype(BF16).astype(F32)
     place = iota((tall, width), 0)
-    bias_rows = jnp.where(place == cap, bias_high, bias_sum - bias_high)
-    bias_rows = jnp.where(place < cap, F32(0.0), bias_rows)
-    message = remote.reshape(-1, tall, width)
-    message = jnp.where((place < cap + hub_own)[None], bias_rows[None], message)
-    message_ref[width:, :] = message.reshape(remote.shape).astype(BF16)
+    bias_rows = jnp.where(place == 0, bias_high, bias_sum - bias_high)
+    hubs = remote.shape[0] // tall * hub_own
+    row = iota((hubs, remote.shape[0]), 0)
+    source = div_floor(row, hub_own) * tall + cap + hub_own + remainder(row, hub_own)
+    wanted = iota(source.shape, 1) == source
+    wanted = jnp.where(wanted, F32(1.0), F32(0.0)).astype(BF16)
+    packed = [matmul(wanted, remote.astype(BF16)), bias_rows, jnp.zeros_like(bias_rows)]
+    message_ref[width:, :] = jnp.concatenate(packed, axis=0).astype(BF16)
     mine = lax.axis_index("side")
     w_own_ref[...] = w_grad_ref[mine]
     message_ref[:width, :] = w_grad_ref[1 - mine].astype(BF16)
@@ -331,21 +334,15 @@
     peers, slab, width = slabs_ref.shape
     total = jnp.sum(slabs_ref[...].astype(F32), axis=0)
     received_ref = received_ref.at[width:, :]
-    size = min(peers * tall, LANES)
-    to, source = iota((size, size), 0), iota((size, size), 1)
+    hubs = peers * hub_own
+    to, source = iota((peers * tall, hubs), 0), iota((peers * tall, hubs), 1)
     entry = remainder(to, tall) - cap
-    moved = (source == to + hub_own) & (entry >= 0) & (entry < hub_own)
+    moved = (source == div_floor(to, tall) * hub_own + entry) & (entry >= 0) & (entry < hub_own)
     moved = jnp.where(moved, F32(1.0), F32(0.0)).astype(BF16)
-    rest = own_ref[...] + jnp.concatenate(
-        [
-            matmul(moved, received_ref[first : first + size, :])
-            for first in range(0, peers * tall, size)
-        ],
-        axis=0,
-    )
+    rest = own_ref[...] + matmul(moved, received_ref[:hubs, :])
     place = iota((tall, width), 0)
-    bias = received_ref[: 2 * tall, :].astype(F32)[:tall, :]
-    bias = jnp.where((place >= cap) & (place < cap + BIAS_ROWS), bias, F32(0.0)) + bias_ref[...]
+    bias = received_ref[hubs:, :].astype(F32)[:tall, :]
+    bias = jnp.where(place < BIAS_ROWS, bias, F32(0.0)) + bias_ref[...]
     bias = jnp.broadcast_to(jnp.sum(bias, axis=0, keepdims=True), (tall, width))
     bias_high = bias.astype(BF16).astype(F32)
     bias_rows = jnp.where(place == tall - 1, bias - bias_high, bias_high)
@@ -507,7 +504,7 @@
             pltpu.HBM((rows, width), BF16),
             shape((width, width), F32),
             shape((slots, width), F32),
-            shape((width + slots, width), BF16),
+            shape((width + peers * hub_own + 2 * tall, width), BF16),
             shape((rows, width), BF16),
             shape((rows, width), BF16),
             shape((8, width), F32),

time: 49.3 us -> 49.4 us (level)
  no operation moved by 1% of the time
where the time goes in v7:
time: 49.4 us; the launch traced here: 49.2 us
  blocking collectives  37.3 us (76%)
  Pallas kernels  9.79 us (20%)
  waiting for transfers between devices  0.76 us (2%)
  between operations  0.7 us (1%)
  starting transfers between devices  0.59 us (1%)
    all_to_all x3, blocking collectives, swap(): return lax.all_to_all(array, axes, split_axis=0, concat_axis=0, tiled=True)  37.3 us
    pallas_call x1, Pallas kernels, on_device(): call(functools.partial(joint_kernel, sizes), (pltpu.HBM((rows, width), BF...  2.63 us
    pallas_call x1, Pallas kernels, on_device(): call(functools.partial(own_kernel, tiles), (shape((width, width), BF16),...  2.18 us
    pallas_call x1, Pallas kernels, on_device(): call(functools.partial(pick_kernel, sizes), (shape((doms * tall, width),...  1.75 us
    pallas_call x1, Pallas kernels, on_device(): call(functools.partial(feat_grad_kernel, sizes, slab), shape((rows, width...  1.21 us
  transfers between devices with their start and end apart: 3, of which 2 were waited for; matrix products, arithmetic and copies ran while one was open for 0% of the time, Pallas kernels for 9%

profile of v7, /device:TPU:0, one launch (start us, length us, event | category | flops | bytes accessed | tf_op | source)
XLA Modules:
  0.0 49.2 jit_solution(16248571104587986912)
XLA Ops:
  0.6 1.8 %shard_map.128 = (bf16[64,256]{1,0:T(8,128)(2,1)S(1)}, bf16[16,256]{1,0:T(8,128)(2,1)S(1)}, s32[1,128]{1,0:T(1,128)S(1)}, bf16[1024,256]{1,0:T(8,128)(2,1)S(1)},...) custom-call(s32[2]{0:T(128)} %hub_hbm.1, ...), custom_call_target="tpu_custom_call" | custom-call | flops 67108864 | bytes 524288 | tf_op jit(solution)/shard_map/pallas_call | solution.py:438
  2.4 0.5 %collective-permute-start = (bf16[16,256]{1,0:T(8,128)(2,1)S(1)}, bf16[16,256]{1,0:T(8,128)(2,1)S(1)}, u32[]{:S(2)}, u32[]{:S(2)}) collective-permute-start(bf16[16,256]{1,0:T(8,128)(2,1)S(1)} %get-tuple-element.37), channel_id=1, source_target_pairs={{0,1},{1,0},{2,3},{3,2},{4,5},{5,4},{6,7},{7,6},{8,9},{9,8},{10,11... | collective-permute-start | bytes 24584 | tf_op jit(solution)/shard_map/ppermute | solution.py:416
  2.9 2.2 %shard_map.129 = (bf16[256,256]{1,0:T(8,128)(2,1)S(1)}, bf16[1024,256]{1,0:T(8,128)(2,1)S(1)}, bf16[256,1024]{1,0:T(8,128)(2,1)S(1)}, f32[256,1024]{1,0:T(8,128)...) custom-call(bf16[1024,256]{1,0:T(8,128)(2,1)S(1)} %get-tuple-element, ...), custom_call_target="tpu_custom_call" | custom-call | flops 2415919104 | bytes 5242880 | tf_op jit(solution)/shard_map/pallas_call | solution.py:474
  5.1 0.0 collective-permute-done.hubs_ref
  5.1 15.2 %all_to_all.21 = bf16[16,8,256]{2,1,0:T(8,128)(2,1)S(1)} all-to-all(bf16[16,8,256]{2,1,0:T(8,128)(2,1)S(1)} %bitcast.8), channel_id=1, replica_groups=mesh['dom'=8,'pair'=2,'side'=2] {'dom','pair'}, dimensions={0} | all-to-all | bytes 131072 | tf_op jit(solution)/shard_map/all_to_all | solution.py:412
  20.4 2.6 %shard_map.131 = (bf16[1024,256]{1,0:T(8,128)(2,1)}, f32[256,256]{1,0:T(8,128)S(1)}, f32[128,256]{1,0:T(8,128)S(1)}, bf16[304,256]{1,0:T(8,128)(2,1)S(1)}, bf16[...) custom-call(bf16[128,256]{1,0:T(8,128)(2,1)S(1)} %bitcast.7, ...), custom_call_target="tpu_custom_call" | custom-call | flops 671088640 | bytes 4194304 | tf_op jit(solution)/shard_map/pallas_call | solution.py:501
  23.0 0.1 collective-permute-start.1
  23.1 0.8 %shard_map.132.after_ref.feat_grad_ref = f32[1024,256]{1,0:T(8,128)S(1)} custom-call(bf16[1024,256]{1,0:T(8,128)(2,1)S(1)} %get-tuple-element.56.low_ref, bf16[256,256]{1,0:T(8,128)(2,1)S(1)} %get-tuple-element.39.w_self_ref, bf16[1024,256]{1,0:T(8,128)(2,1)S(1)} %get-tuple-element.57.edge_grad_ref, bf16[1024,256]{1,0:T(8,128)(2,1)S(1)} %get-tuple-element.42.refs_0_, ...), custom_call_target="tpu_custom_call" | custom-call | flops 671088640 | bytes 2097152 | tf_op jit(solution)/shard_map/pallas_call | solution.py:524
  23.9 0.5 %collective-permute-done.1.received_ref = bf16[304,256]{1,0:T(8,128)(2,1)S(1)} collective-permute-done((bf16[304,256]{1,0:T(8,128)(2,1)S(1)}, bf16[304,256]{1,0:T(8,128)(2,1)S(1)}, u32[]{:S(2)}, u32[]{:S(2)}) %collective-permute-start.1) | collective-permute-done | bytes 155680 | tf_op jit(solution)/shard_map/ppermute | solution.py:416
  24.5 10.6 %all_to_all.22.slabs_ref = bf16[16,16,256]{2,1,0:T(8,128)(2,1)S(1)} all-to-all(bf16[16,16,256]{2,1,0:T(8,128)(2,1)S(1)} %shard_map.133), channel_id=1, replica_groups=mesh['dom'=8,'pair'=2,'side'=2] {'dom','pair'}, dimensions={0} | all-to-all | bytes 262144 | tf_op jit(solution)/shard_map/all_to_all | solution.py:412
  35.1 0.2 shard_map.134
  35.3 11.5 %all_to_all.23.message_ref.mine_ref = bf16[16,24,256]{2,1,0:T(8,128)(2,1)S(1)} all-to-all(bf16[16,24,256]{2,1,0:T(8,128)(2,1)S(1)} %shard_map.134), channel_id=1, replica_groups=mesh['dom'=8,'pair'=2,'side'=2] {'dom','pair'}, dimensions={0} | all-to-all | bytes 393216 | tf_op jit(solution)/shard_map/all_to_all | solution.py:412
  46.8 0.0 collective-permute-start.2
  46.8 1.2 %shard_map.135 = bf16[1024,256]{1,0:T(8,128)(2,1)} custom-call(bf16[16,24,256]{2,1,0:T(8,128)(2,1)S(1)} %all_to_all.23.message_ref.mine_ref, s32[1,128]{1,0:T(1,128)S(1)} %get-tuple-element.63.places_ref, f32[1024,256]{1,0:T(8,128)S(1)} %shard_map.132.after_ref.feat_grad_ref), custom_call_target="tpu_custom_call" | custom-call | flops 134217728 | bytes 1572864 | tf_op jit(solution)/shard_map/pallas_call | solution.py:539
  48.0 0.2 collective-permute-done.2.other_ref
  48.2 1.0 %shard_map.136 = (f32[256,256]{1,0:T(8,128)}, f32[256,256]{1,0:T(8,128)}, f32[1,256]{1,0:T(1,128)}) custom-call(bf16[16,24,256]{2,1,0:T(8,128)(2,1)S(1)} %all_to_all.23.message_ref.mine_ref, bf16[16,24,256]{2,1,0:T(8,128)(2,1)S(1)} %collective-permute-done.2.other_ref), custom_call_target="tpu_custom_call" | custom-call | tf_op jit(solution)/shard_map/pallas_call | solution.py:544
  (2 shorter events, 0.1 us)
Async XLA Ops:
  2.4 2.7 %collective-permute-start = (bf16[16,256]{1,0:T(8,128)(2,1)S(1)}, bf16[16,256]{1,0:T(8,128)(2,1)S(1)}, u32[]{:S(2)}, u32[]{:S(2)}) collective-permute-start(bf16[16,256]{1,0:T(8,128)(2,1)S(1)} %get-tuple-element.37), channel_id=1, source_target_pairs={{0,1},{1,0},{2,3},{3,2},{4,5},{5,4},{6,7},{7,6},{8,9},{9,8},{10,11... | collective-permute-start | bytes 24584 | tf_op jit(solution)/shard_map/ppermute | solution.py:416
  23.0 1.4 %collective-permute-start.1 = (bf16[304,256]{1,0:T(8,128)(2,1)S(1)}, bf16[304,256]{1,0:T(8,128)(2,1)S(1)}, u32[]{:S(2)}, u32[]{:S(2)}) collective-permute-start(bf16[304,256]{1,0:T(8,128)(2,1)S(1)} %get-tuple-element.55), channel_id=1, source_target_pairs={{0,1},{1,0},{2,3},{3,2},{4,5},{5,4},{6,7},{7,6},{8,9},{9,8},{10,11... | collective-permute-start | bytes 466952 | tf_op jit(solution)/shard_map/ppermute | solution.py:416
  46.8 1.4 %collective-permute-start.2 = (bf16[16,24,256]{2,1,0:T(8,128)(2,1)S(1)}, bf16[16,24,256]{2,1,0:T(8,128)(2,1)S(1)}, u32[]{:S(2)}, u32[]{:S(2)}) collective-permute-start(bf16[16,24,256]{2,1,0:T(8,128)(2,1)S(1)} %all_to_all.23.message_ref.mine_ref), channel_id=1, source_target_pairs={{0,1},{1,0},{2,3},{3,2},{4,5},{5,4},{6,7},{7,6},{8,9},{9,8},{10,11... | collective-permute-start | bytes 589832 | tf_op jit(solution)/shard_map/ppermute | solution.py:416
